TPU v7x, 32 devices: a whole 2x2x4 slice. The times are simulated.
32 devices in a mesh: seq: 8 (over y, x, core), chan: 4 (over z).
Axes of the slice: x: 2, y: 2, z: 4, core: 2. Of those that a mesh axis runs over, the one named last changes fastest.
Arguments:
- tokens: bfloat16 [4096, 8192], P('seq'), may hold values from -6 to 6
- proj_weight: bfloat16 [8192, 3, 2048], P('seq', None, 'chan'), may hold values from -0.0625 to 0.0625
- residues: float32 [16, 2048], P(None, 'chan'), may hold values from -1.5 to 1.5
- decay_rates: float32 [16, 2048], P(None, 'chan'), may hold values from 0.00012207031 to 0.05
- skip_gain: float32 [2048], P('chan'), may hold values from -3 to 3
- grad_out: bfloat16 [4096, 2048], P('seq', 'chan'), may hold values from -6 to 6
Outputs:
- gated_output: bfloat16 [4096, 2048], P('seq', 'chan')
- grad_tokens: bfloat16 [4096, 8192], P('seq', 'chan')
All inputs are finite; a program needn't handle non-finite values.
Results may differ from a plain program's by a relative error of at most 0.022.
Values may be sent and summed in bfloat16 or wider, within the bound.
No kernel may reach another device: no remote copies, remote signals or barrier semaphores. Data moves between devices by JAX's collectives and lax.ppermute only.
A program may use at most 128 MiB of HBM per device.

v0:
```python
import math

import jax
import jax.numpy as jnp
from jax import lax
from jax.sharding import PartitionSpec as P


def entering(value, axis, join, neutral):
    count = lax.axis_size(axis)
    place = lax.axis_index(axis)
    ahead = count - 1 - place
    gathered = jax.tree.map(
        lambda a, kind: lax.all_gather(a.astype(kind), axis), value, (jnp.bfloat16, jnp.bfloat16)
    )
    state = jax.tree.map(lambda a, e: jnp.zeros_like(a) + jnp.asarray(e, a.dtype), value, neutral)

    def one(turn, state):
        source = count - 1 - turn
        return join(
            state,
            jax.tree.map(
                lambda a, own: lax.dynamic_index_in_dim(a, source, 0, False).astype(own.dtype),
                gathered,
                value,
            ),
        )

    return lax.fori_loop(0, ahead, one, state)


def entering_2(value, axis, join, neutral):
    count, mine = (lax.axis_size(axis), lax.axis_index(axis))
    pieces = jax.tree.map(lambda part: lax.all_gather(part, axis), value)
    subtotal = jax.tree.map(
        lambda part, zero: jnp.full_like(part, 0) + jnp.asarray(zero, part.dtype), value, neutral
    )

    def turn(position, subtotal):
        longer = join(subtotal, jax.tree.map(lambda part: part[position], pieces))
        return jax.tree.map(lambda new, old: jnp.where(position < mine, new, old), longer, subtotal)

    return lax.fori_loop(0, count - 1, turn, subtotal)


def make_table(block_len):
    dft_len = 2 * block_len
    freq_ids = jnp.arange(dft_len, dtype=jnp.int32)[:, None]
    time_ids = jnp.arange(block_len, dtype=jnp.int32)[None, :]
    phase_ids = freq_ids * time_ids % dft_len
    angles = 2.0 * math.pi / dft_len * phase_ids.astype(jnp.float32)
    return jnp.concatenate([jnp.cos(angles), jnp.sin(angles)], axis=0)


def filter_parts(decay_rates, residues, block_len):
    decay_step = jnp.exp(-decay_rates)
    mode_gain = residues * jnp.sqrt(-jnp.expm1(-2.0 * decay_rates))
    offsets = jnp.arange(block_len, dtype=jnp.float32)
    powers = jnp.exp(-decay_rates[:, None, :] * offsets[None, :, None])
    return (decay_step, mode_gain, powers)


def block_conv(signal, dft_table, spectra, powers, block_len):
    tok_rows, chan_count = signal.shape
    block_count = tok_rows // block_len
    dft_len = 2 * block_len
    pieces = signal.reshape(block_count, block_len, chan_count)
    spectrum = jnp.einsum("ks,bsc->bkc", dft_table, pieces, precision=lax.Precision.HIGHEST)
    sig_cos = spectrum[:, :dft_len]
    sig_sin = spectrum[:, dft_len:]
    filt_cos = spectra[None, :dft_len]
    filt_sin = spectra[None, dft_len:]
    real_part = sig_cos * filt_cos - sig_sin * filt_sin
    imag_part = sig_cos * filt_sin + sig_sin * filt_cos
    joined = jnp.concatenate([real_part, imag_part], axis=1)
    within = jnp.einsum("ks,bkc->bsc", dft_table, joined, precision=lax.Precision.HIGHEST) / dft_len
    block_ends = jnp.einsum(
        "rsc,bsc->brc", powers[:, ::-1], pieces, precision=lax.Precision.HIGHEST
    )
    return (within, block_ends)


def local_states(block_ends, decay_rates, block_len):
    stride_decay = jnp.exp(-decay_rates * block_len)

    def advance(dev_state, block_end):
        return (stride_decay * dev_state + block_end, dev_state)

    final_state, before = lax.scan(advance, jnp.zeros_like(block_ends[0]), block_ends)
    return (before, final_state)


def carried_state(final_state, decay_rates, tok_rows, backward):
    stride_power = jnp.exp(-decay_rates * tok_rows)

    def combine(earlier, later_pair):
        return (earlier[0] * later_pair[0], earlier[1] * later_pair[0] + later_pair[1])

    identity_pair = (jnp.ones_like(stride_power), jnp.zeros_like(stride_power))
    if backward:
        prefix = entering((stride_power, final_state), "seq", combine, identity_pair)
    else:
        prefix = entering_2((stride_power, final_state), "seq", combine, identity_pair)
    return prefix[1]


def causal_filter(
    signal, dft_table, spectra, powers, decay_step, mode_gain, decay_rates, block_len, backward
):
    within, block_ends = block_conv(signal, dft_table, spectra, powers, block_len)
    before, final_state = local_states(block_ends, decay_rates, block_len)
    incoming_dev = carried_state(final_state, decay_rates, signal.shape[0], backward)
    block_ids = jnp.arange(before.shape[0], dtype=jnp.float32)
    lifted = (
        before
        + jnp.exp(-decay_rates[None] * (block_len * block_ids)[:, None, None]) * incoming_dev[None]
    )
    carried = jnp.einsum(
        "rtc,brc->btc",
        powers,
        (mode_gain * decay_step)[None] * lifted,
        precision=lax.Precision.HIGHEST,
    )
    return (within + carried).reshape(signal.shape)


def local(tokens, proj_weight, residues, decay_rates, skip_gain, grad_out):
    tok_rows = tokens.shape[0]
    chan_count = skip_gain.shape[0]
    flat_w = proj_weight.reshape(proj_weight.shape[0], 3 * chan_count)
    whole_w = lax.all_gather(flat_w, "seq", axis=0, tiled=True)
    projected = jnp.dot(tokens, whole_w, preferred_element_type=jnp.float32)
    proj_vals = (
        lax.optimization_barrier(projected.astype(jnp.bfloat16))
        .astype(jnp.float32)
        .reshape(tok_rows, 3, chan_count)
    )
    query_in = proj_vals[:, 0]
    key_in = proj_vals[:, 1]
    value_in = proj_vals[:, 2]
    block_len = min(128, tok_rows)
    dft_table = make_table(block_len)
    decay_step, mode_gain, powers = filter_parts(decay_rates, residues, block_len)
    filter_taps = jnp.einsum("rtc,rc->tc", powers, mode_gain, precision=lax.Precision.HIGHEST)
    spectra = jnp.dot(dft_table, filter_taps, precision=lax.Precision.HIGHEST)
    mixed_in = key_in * value_in
    filtered = causal_filter(
        mixed_in, dft_table, spectra, powers, decay_step, mode_gain, decay_rates, block_len, False
    )
    filtered = filtered + skip_gain[None, :] * mixed_in
    gated_output = (query_in * filtered).astype(jnp.bfloat16)
    grad_gate = grad_out.astype(jnp.float32)
    grad_mix = grad_gate * query_in
    grad_query = grad_gate * filtered
    grad_conv = causal_filter(
        grad_mix[::-1],
        dft_table,
        spectra,
        powers,
        decay_step,
        mode_gain,
        decay_rates,
        block_len,
        True,
    )[::-1]
    grad_conv = grad_conv + skip_gain[None, :] * grad_mix
    grad_proj = jnp.stack([grad_query, grad_conv * value_in, grad_conv * key_in], axis=1).astype(
        jnp.bfloat16
    )
    grad_proj = grad_proj.reshape(tok_rows, 3 * chan_count)
    contract = (((1,), (1,)), ((), ()))
    dx_terms = lax.dot_general(grad_proj, whole_w, contract, preferred_element_type=jnp.float32)
    grad_tokens = lax.psum_scatter(
        dx_terms.astype(jnp.bfloat16), "chan", scatter_dimension=1, tiled=True
    )
    return (gated_output, grad_tokens)


def solution(mesh):
    placed = (
        P("seq", None),
        P("seq", None, "chan"),
        P(None, "chan"),
        P(None, "chan"),
        P("chan"),
        P("seq", "chan"),
    )
    return jax.shard_map(
        local,
        mesh=mesh,
        in_specs=placed,
        out_specs=(P("seq", "chan"), P("seq", "chan")),
        check_vma=False,
    )
```

profile of v0, /device:TPU:0, one launch (start us, length us, event | category | flops | bytes accessed | tf_op | source)
XLA Modules:
  0.0 488.0 jit_solution(2290181295826664484)
XLA Ops:
  7.2 4.7 copy.22
  13.3 3.6 multiply_exponential_fusion
  16.9 7.5 %rev.10 = f32[16,128,512]{1,0,2:T(8,128)} reverse(f32[16,128,512]{1,0,2:T(8,128)} %multiply_exponential_fusion), dimensions={1} | reverse | bytes 8388608 | tf_op jit(solution)/shard_map/rev | solution.py:78
  24.6 1.0 copy.31
  25.6 11.8 %all-gather.2 = bf16[128,512]{1,0:T(8,128)(2,1)} all-gather(bf16[16,512]{1,0:T(8,128)(2,1)S(1)} %get-tuple-element.372), channel_id=4, replica_groups=mesh['seq'=8,'chan'=4] {'seq'}, dimensions={0}, use_global_device_ids=true | all-gather | bytes 147456 | tf_op jit(solution)/shard_map/all_gather | solution.py:14
  37.4 11.4 %all-gather = f32[128,512]{1,0:T(8,128)} all-gather(f32[16,512]{1,0:T(8,128)S(1)} %get-tuple-element.374), channel_id=2, replica_groups=mesh['seq'=8,'chan'=4] {'seq'}, dimensions={0}, use_global_device_ids=true | all-gather | bytes 294912 | tf_op jit(solution)/shard_map/all_gather | solution.py:34
  49.4 4.2 fusion.11
  53.5 1.0 fusion.54
  54.5 1.1 fusion.65
  55.6 86.1 %all-gather.6.cloned.1.call-done = bf16[8192,1536]{0,1:T(8,128)(2,1)} async-done(((bf16[1024,1536]{0,1:T(8,128)(2,1)}), bf16[8192,1536]{0,1:T(8,128)(2,1)}) %all-gather.6.cloned.1.call-update) | async-done | bytes 25165840 | tf_op jit(solution)/shard_map/all_gather | solution.py:131
  141.7 20.1 %convolution_convert_fusion.1 = bf16[512,1536]{1,0:T(8,128)(2,1)} fusion(bf16[512,8192]{1,0:T(8,128)(2,1)} %param.14, bf16[8192,1536]{0,1:T(8,128)(2,1)} %all-gather.6.cloned.1.call-done), kind=kOutput, calls=%fused_computation.22 | convolution fusion | flops 12885688320 | bytes 35127296 | tf_op jit(solution)/shard_map/dot_general | solution.py:132
  161.8 1.9 copy.23
  163.8 1.2 slice_multiply_fusion
  165.0 2.5 mul.231
  167.5 6.8 %convolution_bitcast_fusion.1 = f32[4,512,512]{2,1,0:T(8,128)} fusion(f32[4,128,512]{1,0,2:T(4,128)} %mul.231, f32[256,128]{1,0:T(8,128)S(1)} %get-tuple-element.378, f32[256,128]{1,0:T(8,128)S(1)} %get-tuple-element.379), kind=kOutput, calls=%fused_computation.24 | convolution fusion | flops 1610678272 | bytes 5505024 | tf_op jit(solution)/shard_map/ks,bsc->bkc/dot_general | solution.py:68
  174.3 7.6 %convolution_bitcast_fusion.3 = f32[4,16,512]{1,0,2:T(4,128)} fusion(f32[4,128,512]{1,0,2:T(4,128)S(1)} %copy-done.2, f32[16,128,512]{1,0,2:T(8,128)S(1)} %copy-done), kind=kOutput, calls=%fused_computation.38 | convolution fusion | flops 50331648 | bytes 5373952 | tf_op jit(solution)/shard_map/rsc,bsc->brc/dot_general | solution.py:77
  182.0 2.2 copy.27
  184.8 5.6 %while.55 = (s32[]{:T(128)}, f32[16,512]{1,0:T(8,128)S(1)}, f32[4,16,512]{2,1,0:T(8,128)}, f32[16,512]{1,0:T(8,128)S(1)}, f32[4,16,512]{2,1,0:T(8,128)}, /*index=5*/s32[]{:T(128)}, s32[]{:T(128)}) while((s32[]{:T(128)}, f32[16,512]{1,0:T(8,128)S(1)}, f32[4,16,512]{2,1,0:T(8,128)}, f32[16,512]{1,0:T(8,128)S(1)}, ...), condition=%wide.region_1.2_spmd.clone, body=%wide.region_0.1_spmd.clone.sunk | while | flops 32771 | bytes 197212 | solution.py:89
  185.4 0.8 bitcast_add_fusion.5
  186.8 0.8 bitcast_add_fusion.5
  188.3 0.8 bitcast_add_fusion.5
  189.7 0.8 bitcast_add_fusion.5
  190.4 10.2 %all-gather.1 = f32[128,512]{1,0:T(8,128)} all-gather(f32[16,512]{1,0:T(8,128)S(1)} %get-tuple-element.237), channel_id=3, replica_groups=mesh['seq'=8,'chan'=4] {'seq'}, dimensions={0}, use_global_device_ids=true | all-gather | bytes 294912 | tf_op jit(solution)/shard_map/all_gather | solution.py:34
  200.7 6.1 %while.56 = (s32[]{:T(128)}, f32[16,512]{1,0:T(8,128)S(1)}, s32[]{:T(128)}, f32[8,16,512]{2,1,0:T(8,128)}, f32[8,16,512]{2,1,0:T(8,128)}, /*index=5*/s32[]{:T(128)}, s32[]{:T(128)}) while((s32[]{:T(128)}, f32[16,512]{1,0:T(8,128)S(1)}, s32[]{:T(128)}, f32[8,16,512]{2,1,0:T(8,128)}, f32[8,16,512]{2,1,0:T(8,128)}, ...), condition=%wide.region_3.4_spmd.clone, body=%wide.region_2.3_spmd.clone.sunk | while | flops 32772 | bytes 131173 | solution.py:43
  201.1 0.8 fusion.80
  201.9 0.8 fusion.80
  202.7 0.8 fusion.80
  203.5 0.8 fusion.80
  204.3 0.8 fusion.80
  205.1 0.8 fusion.80
  206.0 0.8 fusion.80
  206.8 1.7 add_multiply_fusion.1
  208.5 2.2 copy.28
  210.7 6.2 %fusion.10 = f32[512,4,128]{2,1,0:T(4,128)} fusion(f32[4,16,512]{1,0,2:T(4,128)} %copy.28, f32[16,512]{0,1:T(8,128)} %copy-done.8), kind=kOutput, calls=%fused_computation.20 | convolution fusion | flops 51380224 | bytes 1212416 | tf_op jit(solution)/shard_map/rtc,brc->btc/dot_general | solution.py:118
  216.8 2.5 copy.29
  219.4 3.2 multiply_subtract_fusion.1
  222.6 3.6 fusion.27
  226.2 2.5 copy.30
  228.8 3.2 fusion.43
  232.0 9.5 %rev.11 = f32[512,512]{0,1:T(8,128)} reverse(f32[512,512]{0,1:T(8,128)} %get-tuple-element.366), dimensions={0} | reverse | bytes 2097152 | tf_op jit(solution)/shard_map/rev | solution.py:156
  241.5 2.5 reshape.51
  244.0 6.8 %convolution_bitcast_fusion = f32[4,512,512]{2,1,0:T(8,128)} fusion(f32[256,128]{1,0:T(8,128)S(1)} %get-tuple-element.378, f32[256,128]{1,0:T(8,128)S(1)} %get-tuple-element.379, f32[512,512]{0,1:T(8,128)} %rev.11), kind=kOutput, calls=%fused_computation.23 | convolution fusion | flops 1610678272 | bytes 5505024 | tf_op jit(solution)/shard_map/ks,bsc->bkc/dot_general | solution.py:68
  250.8 7.7 %convolution_bitcast_fusion.2 = f32[4,16,512]{1,0,2:T(4,128)} fusion(f32[4,128,512]{1,0,2:T(4,128)S(1)} %copy-done.5, f32[16,128,512]{1,0,2:T(8,128)S(1)} %copy-done.1), kind=kOutput, calls=%fused_computation.37 | convolution fusion | flops 50331648 | bytes 5373952 | tf_op jit(solution)/shard_map/rsc,bsc->brc/dot_general | solution.py:77
  258.5 2.2 copy.34
  261.4 5.6 %while.57 = (s32[]{:T(128)}, f32[16,512]{1,0:T(8,128)S(1)}, f32[4,16,512]{2,1,0:T(8,128)}, f32[16,512]{1,0:T(8,128)S(1)}, f32[4,16,512]{2,1,0:T(8,128)}, /*index=5*/s32[]{:T(128)}, s32[]{:T(128)}) while((s32[]{:T(128)}, f32[16,512]{1,0:T(8,128)S(1)}, f32[4,16,512]{2,1,0:T(8,128)}, f32[16,512]{1,0:T(8,128)S(1)}, ...), condition=%wide.region_5.6_spmd.clone, body=%wide.region_4.5_spmd.clone.sunk | while | flops 32771 | bytes 197212 | solution.py:89
  262.0 0.8 bitcast_add_fusion.6
  263.4 0.8 bitcast_add_fusion.6
  264.8 0.8 bitcast_add_fusion.6
  266.2 0.8 bitcast_add_fusion.6
  267.0 9.2 %all-gather.3 = bf16[128,512]{1,0:T(8,128)(2,1)} all-gather(bf16[16,512]{1,0:T(8,128)(2,1)S(1)} %convert_element_type.54), channel_id=5, replica_groups=mesh['seq'=8,'chan'=4] {'seq'}, dimensions={0}, use_global_device_ids=true | all-gather | bytes 147456 | tf_op jit(solution)/shard_map/all_gather | solution.py:14
  276.2 5.2 %while.54 = (s32[]{:T(128)}, f32[16,512]{1,0:T(8,128)S(1)}, s32[]{:T(128)}, bf16[8,16,512]{2,1,0:T(8,128)(2,1)}, bf16[8,16,512]{2,1,0:T(8,128)(2,1)}, /*index=5*/s32[]{:T(128)}, s32[]{:T(128)}, s32[]{:T(128)}, s32[]{:T(128)}) while((s32[]{:T(128)}, f32[16,512]{1,0:T(8,128)S(1)}, s32[]{:T(128)}, bf16[8,16,512]{2,1,0:T(8,128)(2,1)}, ...), condition=%wide.region_7.8_spmd, body=%wide.region_6.7_spmd.sunk | while | flops 32774 | bytes 98447 | solution.py:29
  281.4 1.7 add_multiply_fusion
  283.1 2.3 copy.35
  285.4 6.4 %fusion.9 = f32[512,4,128]{2,1,0:T(4,128)} fusion(f32[4,16,512]{1,0,2:T(4,128)} %copy.35, f32[16,512]{0,1:T(8,128)} %copy-done.8), kind=kOutput, calls=%fused_computation.19 | convolution fusion | flops 51380224 | bytes 1212416 | tf_op jit(solution)/shard_map/rtc,brc->btc/dot_general | solution.py:118
  291.8 2.6 copy.36
  294.3 3.2 multiply_subtract_fusion
  297.6 3.7 fusion.30
  301.3 2.6 copy.37
  303.8 9.3 %rev.12 = f32[512,512]{0,1:T(8,128)} reverse(f32[512,512]{0,1:T(8,128)} %copy.37), dimensions={0} | reverse | bytes 2097152 | tf_op jit(solution)/shard_map/rev | solution.py:155
  313.2 3.2 fusion.42
  316.5 20.6 %convolution_convert_fusion = bf16[512,8192]{1,0:T(8,128)(2,1)} fusion(bf16[512,1536]{0,1:T(8,128)(2,1)S(1)} %bitcast.143, bf16[8192,1536]{0,1:T(8,128)(2,1)} %all-gather.6.cloned.1.call-done), kind=kOutput, calls=%fused_computation.9 | convolution fusion | flops 12889096192 | bytes 35127296 | tf_op jit(solution)/shard_map/dot_general | solution.py:172
  337.2 1.0 copy-done.6
  338.2 1.0 copy.38
  339.2 141.7 %reduce-scatter.2.cloned.1.call-done = bf16[512,2048]{1,0:T(8,128)(2,1)} async-done(((bf16[512,8192]{1,0:T(8,128)(2,1)}), bf16[512,2048]{1,0:T(8,128)(2,1)}) %reduce-scatter.2.cloned.1.call-update) | async-done | bytes 2097168 | tf_op jit(solution)/shard_map/reduce_scatter | solution.py:173
  (63 shorter events, 13.7 us)
Async XLA Ops:
  7.2 4.9 copy-start.14
  7.2 4.9 copy-start.13
  7.2 134.5 %all-gather.6.cloned.1.call-start = ((), (), s32[]{:S(2)}) async-start(), calls=%async_computation.1 | async-start | bytes 28311552 | tf_op jit(solution)/shard_map/all_gather | solution.py:131
  11.9 469.0 %reduce-scatter.2.cloned.1.call-start = ((), (), s32[]{:S(2)}) async-start(), calls=%async_computation.2 | async-start | bytes 10485760 | tf_op jit(solution)/shard_map/reduce_scatter | solution.py:173
  12.7 0.6 copy-start.10
  13.3 36.0 %copy-start.8 = (f32[16,512]{0,1:T(8,128)}, f32[16,512]{0,1:T(8,128)S(1)}, u32[]{:S(2)}) copy-start(f32[16,512]{0,1:T(8,128)S(1)} %copy.25) | copy-start | bytes 98308
  16.9 7.7 %copy-start.9 = (bf16[512,512]{1,0:T(8,128)(2,1)S(1)}, bf16[512,512]{1,0:T(8,128)(2,1)}, u32[]{:S(2)}) copy-start(bf16[512,512]{1,0:T(8,128)(2,1)} %param.19) | copy-start | bytes 1572868
  167.5 6.8 %copy-start = (f32[16,128,512]{1,0,2:T(8,128)S(1)}, f32[16,128,512]{1,0,2:T(8,128)}, u32[]{:S(2)}) copy-start(f32[16,128,512]{1,0,2:T(8,128)} %rev.10) | copy-start | bytes 12582916
  167.5 6.8 %copy-start.2 = (f32[4,128,512]{1,0,2:T(4,128)S(1)}, f32[4,128,512]{1,0,2:T(4,128)}, u32[]{:S(2)}) copy-start(f32[4,128,512]{1,0,2:T(4,128)} %mul.231) | copy-start | bytes 3145732
  219.4 3.2 copy-start.4
  222.6 6.2 %copy-start.15 = (f32[512]{0:T(512)S(1)}, f32[512]{0:T(512)}, u32[]{:S(2)}) copy-start(f32[512]{0:T(512)} %param.18) | copy-start | bytes 6148
  244.0 6.8 %copy-start.1 = (f32[16,128,512]{1,0,2:T(8,128)S(1)}, f32[16,128,512]{1,0,2:T(8,128)}, u32[]{:S(2)}) copy-start(f32[16,128,512]{1,0,2:T(8,128)} %rev.10) | copy-start | bytes 12582916
  244.0 6.8 %copy-start.5 = (f32[4,128,512]{1,0,2:T(4,128)S(1)}, f32[4,128,512]{1,0,2:T(4,128)}, u32[]{:S(2)}) copy-start(f32[4,128,512]{1,0,2:T(4,128)} %reshape.51) | copy-start | bytes 3145732
  250.8 30.6 %copy-start.11 = (f32[16,512]{1,0:T(8,128)S(1)}, f32[16,512]{1,0:T(8,128)}, u32[]{:S(2)}) copy-start(f32[16,512]{1,0:T(8,128)} %copy-done.10) | copy-start | bytes 98308
  250.8 30.6 %copy-start.12 = (f32[16,512]{1,0:T(8,128)S(1)}, f32[16,512]{1,0:T(8,128)}, u32[]{:S(2)}) copy-start(f32[16,512]{1,0:T(8,128)} %get-tuple-element.376) | copy-start | bytes 98308
  294.3 3.2 copy-start.3
  313.2 3.2 copy-start.7
  337.2 1.0 copy-start.6
Sparse Core Ops, SparseCore 0:
  12.1 129.5 all-gather.5
  337.3 143.5 reduce-scatter.1
where the time goes:
time: 494 us; the launch traced here: 488 us
  waiting for transfers between devices  228 us (46%)
  matrix products  94.7 us (19%)
  local copies, waits for them, and re-layouts  63.3 us (13%)
  other arithmetic  44.1 us (9%)
  blocking collectives  42.7 us (9%)
  between operations  14.5 us (3%)
    reduce_scatter x1, waiting for transfers between devices, local(): lax.psum_scatter(dx_terms.astype(jnp.bfloat16), 'chan', scatter_dimension...  142 us
    all_gather x1, waiting for transfers between devices, local(): whole_w = lax.all_gather(flat_w, 'seq', axis=0, tiled=True)  86.1 us
    all_gather x2, blocking collectives, entering_2(): pieces = jax.tree.map(lambda part: lax.all_gather(part, axis), value)  21.7 us
    all_gather x2, blocking collectives, entering(): lax.all_gather(a.astype(kind), axis)  21 us
    dot_general x1, matrix products, local(): lax.dot_general(grad_proj, whole_w, contract, preferred_element_type=jnp....  20.6 us
    dot_general x1, matrix products, local(): projected = jnp.dot(tokens, whole_w, preferred_element_type=jnp.float32)  20.1 us
    dot_general x2, matrix products, block_conv(): jnp.einsum('rsc,bsc->brc', powers[:, ::-1], pieces, precision=lax.Precisi...  15.3 us
    dot_general x2, matrix products, block_conv(): jnp.einsum('ks,bsc->bkc', dft_table, pieces, precision=lax.Precision.HIGH...  13.6 us
  transfers between devices with their start and end apart: 2, of which 2 were waited for; matrix products, arithmetic and copies ran while one was open for 4% of the time, Pallas kernels for 0%

commit v1 on v0

v1 whole, which is shorter than its diff:
```python
import functools

import jax
import jax.numpy as jnp
from jax import lax
from jax.experimental import pallas as pl
from jax.experimental.pallas import tpu as pltpu
from jax.sharding import PartitionSpec as P

LANES = 128
SUBS = 8
MODES = 16
BLOCKS = 8
VMEM_BYTES = 48 * 1024 * 1024


def coefficients(residues, decay_rates, rows):
    return jnp.stack(
        [
            jnp.exp(-decay_rates),
            residues * jnp.sqrt(-jnp.expm1(-2.0 * decay_rates)),
            jnp.exp(-decay_rates * (rows // SUBS)),
            jnp.exp(-decay_rates * rows),
        ]
    )


def spread(coef_ref, which):
    table = coef_ref[which]
    return [jnp.broadcast_to(table[r : r + 1, :], (SUBS, LANES)) for r in range(MODES)]


def end_states(signal_ref, decay, run, backward):
    def step(j, state):
        at = run - 1 - j if backward else j
        row = signal_ref[pl.ds(at, SUBS, stride=run), :]
        return tuple(a * s + row for a, s in zip(decay, state))

    zero = jnp.zeros((SUBS, LANES), jnp.float32)
    return lax.fori_loop(0, run, step, (zero,) * MODES, unroll=8)


def full_scan(signal_ref, out_ref, decay, gain, state, run, backward):
    def step(j, state):
        at = run - 1 - j if backward else j
        rows = pl.ds(at, SUBS, stride=run)
        row = signal_ref[rows, :]
        state = tuple(a * s + row for a, s in zip(decay, state))
        terms = [g * s for g, s in zip(gain, state)]
        while len(terms) > 1:
            terms = [terms[i] + terms[i + 1] for i in range(0, len(terms), 2)]
        out_ref[rows, :] = terms[0]
        return state

    lax.fori_loop(0, run, step, tuple(state), unroll=8)


def project_kernel(run, order_ref, x_ref, w_ref, g_ref, coef_ref, proj_ref, runs_ref, ends_ref, acc, mix, gmix):
    k = pl.program_id(0)

    @pl.when(k == 0)
    def _():
        acc[...] = jnp.zeros_like(acc)

    x = x_ref[...]
    w = jnp.concatenate([w_ref[0, b] for b in range(3)], axis=1)
    acc[...] += jnp.dot(x, w, preferred_element_type=jnp.float32)

    @pl.when(k == pl.num_programs(0) - 1)
    def _():
        for b in range(3):
            proj_ref[b] = acc[:, b * LANES : (b + 1) * LANES].astype(jnp.bfloat16)
        mix[...] = proj_ref[1].astype(jnp.float32) * proj_ref[2].astype(jnp.float32)
        gmix[...] = g_ref[...].astype(jnp.float32) * proj_ref[0].astype(jnp.float32)
        decay = spread(coef_ref, 0)
        long = coef_ref[2]
        for way, signal in enumerate((mix, gmix)):
            state = end_states(signal, decay, run, way == 1)
            for r in range(MODES):
                runs_ref[way, pl.ds(r, SUBS, stride=MODES), :] = state[r]
            total = jnp.zeros((MODES, LANES), jnp.float32)
            for i in range(SUBS):
                at = SUBS - 1 - i if way else i
                total = long * total + runs_ref[way, at * MODES : (at + 1) * MODES, :]
            ends_ref[way] = total


def scan_kernel(run, place_ref, proj_ref, g_ref, coef_ref, skip_ref, runs_ref, ends_ref, gated_ref, gp_ref, mix, out, start):
    me = place_ref[0]
    count = ends_ref.shape[0]
    decay = spread(coef_ref, 0)
    gain = spread(coef_ref, 1)
    long = coef_ref[2]
    whole = coef_ref[3]
    skip = skip_ref[...]
    grad = g_ref[...].astype(jnp.float32)
    query = proj_ref[0].astype(jnp.float32)
    for way in range(2):
        state = jnp.zeros((MODES, LANES), jnp.float32)
        for i in range(count - 1):
            at = count - 1 - i if way else i
            keep = me < at if way else at < me
            state = jnp.where(keep, whole * state + ends_ref[at, way], state)
        for i in range(SUBS):
            at = SUBS - 1 - i if way else i
            start[at * MODES : (at + 1) * MODES, :] = state
            state = long * state + runs_ref[way, at * MODES : (at + 1) * MODES, :]
        first = [start[pl.ds(r, SUBS, stride=MODES), :] for r in range(MODES)]
        if way:
            mix[...] = grad * query
        else:
            mix[...] = proj_ref[1].astype(jnp.float32) * proj_ref[2].astype(jnp.float32)
        full_scan(mix, out, decay, gain, first, run, way == 1)
        filtered = out[...] + skip * mix[...]
        if way:
            gp_ref[:, LANES : 2 * LANES] = (filtered * proj_ref[2].astype(jnp.float32)).astype(jnp.bfloat16)
            gp_ref[:, 2 * LANES : 3 * LANES] = (filtered * proj_ref[1].astype(jnp.float32)).astype(jnp.bfloat16)
        else:
            gated_ref[...] = (query * filtered).astype(jnp.bfloat16)
            gp_ref[:, :LANES] = (grad * filtered).astype(jnp.bfloat16)


def project(order, tokens, pieces, grad_out, coef, chunk):
    rows, width = tokens.shape
    depth = width // BLOCKS
    run = rows // SUBS
    return pl.pallas_call(
        functools.partial(project_kernel, run),
        grid_spec=pltpu.PrefetchScalarGridSpec(
            num_scalar_prefetch=1,
            grid=(BLOCKS,),
            in_specs=[
                pl.BlockSpec((rows, depth), lambda k, order: (0, order[k])),
                pl.BlockSpec((1, 3, depth, LANES), lambda k, order: (k, 0, 0, 0)),
                pl.BlockSpec((rows, LANES), lambda k, order: (0, chunk)),
                pl.BlockSpec((4, MODES, LANES), lambda k, order: (0, 0, chunk)),
            ],
            out_specs=[
                pl.BlockSpec((3, rows, LANES), lambda k, order: (0, 0, 0)),
                pl.BlockSpec((2, SUBS * MODES, LANES), lambda k, order: (0, 0, 0)),
                pl.BlockSpec((2, MODES, LANES), lambda k, order: (0, 0, 0)),
            ],
            scratch_shapes=[
                pltpu.VMEM((rows, 3 * LANES), jnp.float32),
                pltpu.VMEM((rows, LANES), jnp.float32),
                pltpu.VMEM((rows, LANES), jnp.float32),
            ],
        ),
        out_shape=[
            jax.ShapeDtypeStruct((3, rows, LANES), jnp.bfloat16),
            jax.ShapeDtypeStruct((2, SUBS * MODES, LANES), jnp.float32),
            jax.ShapeDtypeStruct((2, MODES, LANES), jnp.float32),
        ],
        compiler_params=pltpu.CompilerParams(vmem_limit_bytes=VMEM_BYTES),
        cost_estimate=pl.CostEstimate(
            flops=2 * rows * width * 3 * LANES, bytes_accessed=2 * width * (rows + 3 * LANES), transcendentals=0
        ),
        name="project",
    )(order, tokens, pieces, grad_out, coef)


def scan(place, proj, grad_out, coef, skip, runs, ends, chunk):
    _, rows, _ = proj.shape
    run = rows // SUBS
    count = ends.shape[0]
    return pl.pallas_call(
        functools.partial(scan_kernel, run),
        grid_spec=pltpu.PrefetchScalarGridSpec(
            num_scalar_prefetch=1,
            grid=(1,),
            in_specs=[
                pl.BlockSpec((3, rows, LANES), lambda k, place: (0, 0, 0)),
                pl.BlockSpec((rows, LANES), lambda k, place: (0, chunk)),
                pl.BlockSpec((4, MODES, LANES), lambda k, place: (0, 0, chunk)),
                pl.BlockSpec((1, LANES), lambda k, place: (0, chunk)),
                pl.BlockSpec((2, SUBS * MODES, LANES), lambda k, place: (0, 0, 0)),
                pl.BlockSpec((count, 2, MODES, LANES), lambda k, place: (0, 0, 0, 0)),
            ],
            out_specs=[
                pl.BlockSpec((rows, LANES), lambda k, place: (0, 0)),
                pl.BlockSpec((rows, 3 * LANES), lambda k, place: (0, 0)),
            ],
            scratch_shapes=[
                pltpu.VMEM((rows, LANES), jnp.float32),
                pltpu.VMEM((rows, LANES), jnp.float32),
                pltpu.VMEM((SUBS * MODES, LANES), jnp.float32),
            ],
        ),
        out_shape=[
            jax.ShapeDtypeStruct((rows, LANES), jnp.bfloat16),
            jax.ShapeDtypeStruct((rows, 3 * LANES), jnp.bfloat16),
        ],
        compiler_params=pltpu.CompilerParams(vmem_limit_bytes=VMEM_BYTES),
        cost_estimate=pl.CostEstimate(flops=rows * LANES * MODES * 16, bytes_accessed=12 * rows * LANES, transcendentals=0),
        name="scan",
    )(place, proj, grad_out, coef, skip, runs, ends)


def input_grad_kernel(chunks, *refs):
    grads, weights, out_ref = refs[:chunks], refs[chunks : 2 * chunks], refs[-1]
    left = jnp.concatenate([g[...] for g in grads], axis=1)
    right = jnp.concatenate([w[0, b] for w in weights for b in range(3)], axis=1)
    total = lax.dot_general(left, right, (((1,), (1,)), ((), ())), preferred_element_type=jnp.float32)
    out_ref[...] = total.astype(out_ref.dtype)


def input_grad(grads, weights, first, stride, count):
    chunks = len(grads)
    rows = grads[0].shape[0]
    depth = weights[0].shape[2]
    return pl.pallas_call(
        functools.partial(input_grad_kernel, chunks),
        grid=(count,),
        in_specs=[pl.BlockSpec((rows, 3 * LANES), lambda i: (0, 0))] * chunks
        + [pl.BlockSpec((1, 3, depth, LANES), lambda i: (first + stride * i, 0, 0, 0))] * chunks,
        out_specs=pl.BlockSpec((rows, depth), lambda i: (0, i)),
        out_shape=jax.ShapeDtypeStruct((rows, count * depth), jnp.bfloat16),
        compiler_params=pltpu.CompilerParams(vmem_limit_bytes=VMEM_BYTES),
        cost_estimate=pl.CostEstimate(
            flops=2 * rows * count * depth * chunks * 3 * LANES,
            bytes_accessed=2 * count * depth * (rows + chunks * 3 * LANES),
            transcendentals=0,
        ),
        name="input_grad",
    )(*grads, *weights)


def gather_chunk(part):
    whole = lax.all_gather(part, "seq")
    count, _, depth, _ = whole.shape
    if count != BLOCKS:
        whole = whole.reshape(BLOCKS, count // BLOCKS, 3, depth, LANES).swapaxes(1, 2)
        whole = whole.reshape(BLOCKS, 3, count // BLOCKS * depth, LANES)
    return whole


def local(tokens, proj_weight, residues, decay_rates, skip_gain, grad_out):
    rows = tokens.shape[0]
    chunks = skip_gain.shape[0] // LANES
    place = lax.axis_index("seq").astype(jnp.int32).reshape(1)
    order = jnp.arange(BLOCKS, dtype=jnp.int32)
    coef = coefficients(residues, decay_rates, rows)
    skip = skip_gain[None, :]
    branches = proj_weight.swapaxes(0, 1)
    weights, gated, grads = [], [], []
    for c in range(chunks):
        whole = gather_chunk(branches[:, :, c * LANES : (c + 1) * LANES])
        weights.append(whole)
        proj, runs, ends = project(order, tokens, whole, grad_out, coef, c)
        ends = lax.all_gather(ends, "seq")
        gate, grad = scan(place, proj, grad_out, coef, skip, runs, ends, c)
        gated.append(gate)
        grads.append(grad)
    halves = []
    for h in range(2):
        dx = input_grad(grads, weights, h, 2, BLOCKS // 2)
        halves.append(lax.psum_scatter(dx, "chan", scatter_dimension=1, tiled=True))
    return (jnp.concatenate(gated, axis=1), jnp.concatenate(halves, axis=1))


def solution(mesh):
    placed = (
        P("seq", None),
        P("seq", None, "chan"),
        P(None, "chan"),
        P(None, "chan"),
        P("chan"),
        P("seq", "chan"),
    )
    return jax.shard_map(
        local,
        mesh=mesh,
        in_specs=placed,
        out_specs=(P("seq", "chan"), P("seq", "chan")),
        check_vma=False,
    )
```

time: 494 us -> 411 us (0.83); the launches traced: 488 us -> 410 us
  matrix products: 94.7 us -> 0 us
  Pallas kernels: 0 us -> 73.9 us
  local copies, waits for them, and re-layouts: 63.3 us -> 7.63 us
  waiting for transfers between devices: 228 us -> 272 us
  other arithmetic: 44.1 us -> 3.99 us
  blocking collectives: 42.7 us -> 37.6 us
    dot_general x12 -> x0, matrix products: 94.7 us -> none  [the longest x1 20.6 us: local(): lax.dot_general(grad_proj, whole_w, contract, preferred_element_type=jnp....]
    pallas_call x0 -> x10, Pallas kernels: none -> 73.9 us  [the longest x4 46.8 us: project(): pl.pallas_call(functools.partial(project_kernel, run), grid_spec=pltpu.Pr...]
    all_gather x1 -> x4, waiting for transfers between devices: 86.1 us -> 127 us  [gather_chunk(): whole = lax.all_gather(part, 'seq')]
    rev x3 -> x0, local copies, waits for them, and re-layouts: 26.4 us -> none  [the longest x1 9.49 us: local(): grad_mix[::-1]]
    add x15 -> x0, other arithmetic: 11.3 us -> none  [the longest x8 6.14 us: advance(): return (stride_decay * dev_state + block_end, dev_state)]
    reshape x4 -> x0, local copies, waits for them, and re-layouts: 9.58 us -> none  [the longest x2 5.11 us: causal_filter(): return (within + carried).reshape(signal.shape)]
    unnamed x37 -> x12, local copies, waits for them, and re-layouts: 12.6 us -> 3.94 us
    mul x4 -> x0, local copies, waits for them, and re-layouts: 7.13 us -> none  [the longest x2 4.47 us: causal_filter(): (mode_gain * decay_step)[None] * lifted]
  transfers between devices with their start and end apart: 2 -> 6, of which waited for: 2 -> 6; matrix products, arithmetic and copies ran while one was open for 4% -> 0% of each run, Pallas kernels for 0% -> 11%
where the time goes in v1:
time: 411 us; the launch traced here: 410 us
  waiting for transfers between devices  272 us (66%)
  Pallas kernels  73.9 us (18%)
  blocking collectives  37.6 us (9%)
  between operations  14.3 us (3%)
  local copies, waits for them, and re-layouts  7.63 us (2%)
    reduce_scatter x2, waiting for transfers between devices, local(): halves.append(lax.psum_scatter(dx, 'chan', scatter_dimension=1, tiled=True))  144 us
    all_gather x4, waiting for transfers between devices, gather_chunk(): whole = lax.all_gather(part, 'seq')  127 us
    pallas_call x4, Pallas kernels, project(): pl.pallas_call(functools.partial(project_kernel, run), grid_spec=pltpu.Pr...  46.8 us
    all_gather x4, blocking collectives, local(): ends = lax.all_gather(ends, 'seq')  37.6 us
    pallas_call x2, Pallas kernels, input_grad(): pl.pallas_call(functools.partial(input_grad_kernel, chunks), grid=(count,...  19.4 us
  transfers between devices with their start and end apart: 6, of which 6 were waited for; matrix products, arithmetic and copies ran while one was open for 0% of the time, Pallas kernels for 11%

profile of v1, /device:TPU:0, one launch (start us, length us, event | category | flops | bytes accessed | tf_op | source)
XLA Modules:
  0.0 410.2 jit_solution(17926742969680149944)
XLA Ops:
  7.2 0.0 all-gather.19.cloned.1.call-start
  7.2 0.0 copy-start.4
  7.2 0.0 copy-start.5
  7.2 0.0 copy-start
  7.2 3.7 fusion
  10.9 0.0 all-gather.19.cloned.1.call-update
  10.9 0.0 all-gather.17.cloned.1.call-start
  11.0 0.7 all-gather.17.cloned.1.call-update
  11.7 0.0 all-gather.15.cloned.1.call-start
  11.7 0.7 all-gather.15.cloned.1.call-update
  12.4 0.0 all-gather.13.cloned.1.call-start
  12.5 0.5 all-gather.13.cloned.1.call-update
  13.0 0.0 reduce-scatter.5.cloned.1.call-start
  13.1 0.0 copy-done.4
  13.1 0.0 copy-done.5
  13.2 46.2 %all-gather.19.cloned.1.call-done = bf16[24,1024,128]{2,1,0:T(8,128)(2,1)} async-done(((bf16[3,1024,128]{2,1,0:T(8,128)(2,1)}), bf16[24,1024,128]{2,1,0:T(8,128)(2,1)}) %all-gather.19.cloned.1.call-update) | async-done | bytes 6291472 | tf_op jit(solution)/shard_map/all_gather | solution.py:229
  59.3 0.0 copy-done
  59.3 11.8 %project.7 = (bf16[3,512,128]{2,1,0:T(8,128)(2,1)S(1)}, f32[2,128,128]{2,1,0:T(8,128)S(1)}, f32[2,16,128]{2,1,0:T(8,128)S(1)}) custom-call(s32[8]{0:T(128)S(1)} %iota.12.order_ref, bf16[512,8192]{1,0:T(8,128)(2,1)} %x_ref.7, bf16[8,3,1024,128]{3,2,1,0:T(8,128)(2,1)} %bitcast.27, bf16[512,512]{1,0:T(8,128)(2,1)S(1)} %copy-done, ...), custom_call_target="tpu_custom_call" | custom-call | flops 3221225472 | bytes 14680064 | tf_op jit(solution)/shard_map/project/pallas_call | solution.py:127
  71.1 9.5 %all-gather.7 = f32[16,16,128]{2,1,0:T(8,128)S(1)} all-gather(f32[2,16,128]{2,1,0:T(8,128)S(1)} %get-tuple-element.36), channel_id=9, replica_groups=mesh['seq'=8,'chan'=4] {'seq'}, dimensions={0}, use_global_device_ids=true | all-gather | bytes 147456 | tf_op jit(solution)/shard_map/all_gather | solution.py:250
  80.6 26.7 %all-gather.17.cloned.1.call-done = bf16[24,1024,128]{2,1,0:T(8,128)(2,1)} async-done(((bf16[3,1024,128]{2,1,0:T(8,128)(2,1)}), bf16[24,1024,128]{2,1,0:T(8,128)(2,1)}) %all-gather.17.cloned.1.call-update) | async-done | bytes 6291472 | tf_op jit(solution)/shard_map/all_gather | solution.py:229
  107.3 11.8 %project.6 = (bf16[3,512,128]{2,1,0:T(8,128)(2,1)S(1)}, f32[2,128,128]{2,1,0:T(8,128)S(1)}, f32[2,16,128]{2,1,0:T(8,128)S(1)}) custom-call(s32[8]{0:T(128)S(1)} %iota.11.order_ref, bf16[512,8192]{1,0:T(8,128)(2,1)} %x_ref.7, bf16[8,3,1024,128]{3,2,1,0:T(8,128)(2,1)} %bitcast.30, bf16[512,512]{1,0:T(8,128)(2,1)S(1)} %copy-done, ...), custom_call_target="tpu_custom_call" | custom-call | flops 3221225472 | bytes 14680064 | tf_op jit(solution)/shard_map/project/pallas_call | solution.py:127
  119.1 9.5 %all-gather.5 = f32[16,16,128]{2,1,0:T(8,128)S(1)} all-gather(f32[2,16,128]{2,1,0:T(8,128)S(1)} %get-tuple-element.32), channel_id=7, replica_groups=mesh['seq'=8,'chan'=4] {'seq'}, dimensions={0}, use_global_device_ids=true | all-gather | bytes 147456 | tf_op jit(solution)/shard_map/all_gather | solution.py:250
  128.5 26.7 %all-gather.15.cloned.1.call-done = bf16[24,1024,128]{2,1,0:T(8,128)(2,1)} async-done(((bf16[3,1024,128]{2,1,0:T(8,128)(2,1)}), bf16[24,1024,128]{2,1,0:T(8,128)(2,1)}) %all-gather.15.cloned.1.call-update) | async-done | bytes 6291472 | tf_op jit(solution)/shard_map/all_gather | solution.py:229
  155.3 11.7 %project.5 = (bf16[3,512,128]{2,1,0:T(8,128)(2,1)S(1)}, f32[2,128,128]{2,1,0:T(8,128)S(1)}, f32[2,16,128]{2,1,0:T(8,128)S(1)}) custom-call(s32[8]{0:T(128)S(1)} %iota.10.order_ref, bf16[512,8192]{1,0:T(8,128)(2,1)} %x_ref.7, bf16[8,3,1024,128]{3,2,1,0:T(8,128)(2,1)} %bitcast.33, bf16[512,512]{1,0:T(8,128)(2,1)S(1)} %copy-done, ...), custom_call_target="tpu_custom_call" | custom-call | flops 3221225472 | bytes 14680064 | tf_op jit(solution)/shard_map/project/pallas_call | solution.py:127
  167.0 9.5 %all-gather.3 = f32[16,16,128]{2,1,0:T(8,128)S(1)} all-gather(f32[2,16,128]{2,1,0:T(8,128)S(1)} %get-tuple-element.28), channel_id=5, replica_groups=mesh['seq'=8,'chan'=4] {'seq'}, dimensions={0}, use_global_device_ids=true | all-gather | bytes 147456 | tf_op jit(solution)/shard_map/all_gather | solution.py:250
  176.5 27.2 %all-gather.13.cloned.1.call-done = bf16[24,1024,128]{2,1,0:T(8,128)(2,1)} async-done(((bf16[3,1024,128]{2,1,0:T(8,128)(2,1)}), bf16[24,1024,128]{2,1,0:T(8,128)(2,1)}) %all-gather.13.cloned.1.call-update) | async-done | bytes 6291472 | tf_op jit(solution)/shard_map/all_gather | solution.py:229
  203.7 0.0 copy-start.3
  203.7 11.5 %project.4 = (bf16[3,512,128]{2,1,0:T(8,128)(2,1)S(1)}, f32[2,128,128]{2,1,0:T(8,128)S(1)}, f32[2,16,128]{2,1,0:T(8,128)S(1)}) custom-call(s32[8]{0:T(128)S(1)} %iota.9.order_ref, bf16[512,8192]{1,0:T(8,128)(2,1)} %x_ref.7, bf16[8,3,1024,128]{3,2,1,0:T(8,128)(2,1)} %bitcast.36, bf16[512,512]{1,0:T(8,128)(2,1)S(1)} %copy-done, ...), custom_call_target="tpu_custom_call" | custom-call | flops 3221225472 | bytes 14680064 | tf_op jit(solution)/shard_map/project/pallas_call | solution.py:127
  215.2 9.2 %all-gather.1 = f32[16,16,128]{2,1,0:T(8,128)S(1)} all-gather(f32[2,16,128]{2,1,0:T(8,128)S(1)} %get-tuple-element.24), channel_id=3, replica_groups=mesh['seq'=8,'chan'=4] {'seq'}, dimensions={0}, use_global_device_ids=true | all-gather | bytes 147456 | tf_op jit(solution)/shard_map/all_gather | solution.py:250
  224.4 0.0 copy-done.3
  224.4 1.9 scan.7
  226.4 1.9 scan.6
  228.3 1.9 scan.5
  230.3 2.0 scan.4
  232.2 9.5 %input_grad.3 = bf16[512,4096]{1,0:T(8,128)(2,1)S(1)} custom-call(bf16[512,384]{1,0:T(8,128)(2,1)S(1)} %get-tuple-element.38.refs_0_, bf16[512,384]{1,0:T(8,128)(2,1)S(1)} %get-tuple-element.39.refs_1_, bf16[512,384]{1,0:T(8,128)(2,1)S(1)} %get-tuple-element.40.refs_2_, bf16[512,384]{1,0:T(8,128)(2,1)S(1)} %get-tuple-element.41.refs_3_, ...), custom_call_target="tpu_custom_call" | custom-call | flops 6442450944 | bytes 16777216 | tf_op jit(solution)/shard_map/input_grad/pallas_call | solution.py:211
  241.7 0.0 copy-start.1
  241.7 2.0 copy-done.1
  243.7 0.0 reduce-scatter.5.cloned.1.call-update
  243.7 0.0 reduce-scatter.3.cloned.1.call-start
  243.8 9.9 %input_grad.2 = bf16[512,4096]{1,0:T(8,128)(2,1)S(1)} custom-call(bf16[512,384]{1,0:T(8,128)(2,1)S(1)} %get-tuple-element.38.refs_0_, bf16[512,384]{1,0:T(8,128)(2,1)S(1)} %get-tuple-element.39.refs_1_, bf16[512,384]{1,0:T(8,128)(2,1)S(1)} %get-tuple-element.40.refs_2_, bf16[512,384]{1,0:T(8,128)(2,1)S(1)} %get-tuple-element.41.refs_3_, ...), custom_call_target="tpu_custom_call" | custom-call | flops 6442450944 | bytes 16777216 | tf_op jit(solution)/shard_map/input_grad/pallas_call | solution.py:211
  253.7 0.0 copy-start.2
  253.7 1.9 copy-done.2
  255.6 0.0 reduce-scatter.3.cloned.1.call-update
  255.7 0.9 pad_maximum_fusion.1
  256.5 64.2 %reduce-scatter.5.cloned.1.call-done = bf16[512,1024]{1,0:T(8,128)(2,1)} async-done(((bf16[512,4096]{1,0:T(8,128)(2,1)}), bf16[512,1024]{1,0:T(8,128)(2,1)}) %reduce-scatter.5.cloned.1.call-update) | async-done | bytes 1048592 | tf_op jit(solution)/shard_map/reduce_scatter | solution.py:257
  320.7 79.5 %reduce-scatter.3.cloned.1.call-done = bf16[512,1024]{1,0:T(8,128)(2,1)} async-done(((bf16[512,4096]{1,0:T(8,128)(2,1)}), bf16[512,1024]{1,0:T(8,128)(2,1)}) %reduce-scatter.3.cloned.1.call-update) | async-done | bytes 1048592 | tf_op jit(solution)/shard_map/reduce_scatter | solution.py:257
  400.2 3.1 pad_maximum_fusion
  (6 shorter events, 0.1 us)
Async XLA Ops:
  7.2 52.2 %all-gather.19.cloned.1.call-start = ((), (), s32[]{:S(2)}) async-start(), calls=%async_computation.7 | async-start | bytes 7077888 | tf_op jit(solution)/shard_map/all_gather | solution.py:229
  7.2 5.9 %copy-start.4 = (f32[16,512]{1,0:T(8,128)S(1)}, f32[16,512]{1,0:T(8,128)}, u32[]{:S(2)}) copy-start(f32[16,512]{1,0:T(8,128)} %param.9) | copy-start | bytes 98308
  7.2 5.9 %copy-start.5 = (f32[16,512]{1,0:T(8,128)S(1)}, f32[16,512]{1,0:T(8,128)}, u32[]{:S(2)}) copy-start(f32[16,512]{1,0:T(8,128)} %param.8) | copy-start | bytes 98308
  7.2 52.1 %copy-start = (bf16[512,512]{1,0:T(8,128)(2,1)S(1)}, bf16[512,512]{1,0:T(8,128)(2,1)}, u32[]{:S(2)}) copy-start(bf16[512,512]{1,0:T(8,128)(2,1)} %g_ref.15) | copy-start | bytes 1572868
  10.9 96.3 %all-gather.17.cloned.1.call-start = ((), (), s32[]{:S(2)}) async-start(), calls=%async_computation.6 | async-start | bytes 7077888 | tf_op jit(solution)/shard_map/all_gather | solution.py:229
  11.7 143.6 %all-gather.15.cloned.1.call-start = ((), (), s32[]{:S(2)}) async-start(), calls=%async_computation.5 | async-start | bytes 7077888 | tf_op jit(solution)/shard_map/all_gather | solution.py:229
  12.4 191.2 %all-gather.13.cloned.1.call-start = ((), (), s32[]{:S(2)}) async-start(), calls=%async_computation.4 | async-start | bytes 7077888 | tf_op jit(solution)/shard_map/all_gather | solution.py:229
  13.0 307.7 %reduce-scatter.5.cloned.1.call-start = ((), (), s32[]{:S(2)}) async-start(), calls=%async_computation.3 | async-start | bytes 5242880 | tf_op jit(solution)/shard_map/reduce_scatter | solution.py:257
  203.7 20.7 %copy-start.3 = (f32[512]{0:T(512)S(1)}, f32[512]{0:T(512)}, u32[]{:S(2)}) copy-start(f32[512]{0:T(512)} %param.10) | copy-start | bytes 6148
  241.7 2.0 copy-start.1
  243.7 156.5 %reduce-scatter.3.cloned.1.call-start = ((), (), s32[]{:S(2)}) async-start(), calls=%async_computation.2 | async-start | bytes 5242880 | tf_op jit(solution)/shard_map/reduce_scatter | solution.py:257
  253.7 1.9 copy-start.2
Sparse Core Ops, SparseCore 0:
  11.1 48.2 all-gather.18
  61.2 46.0 all-gather.16
  109.2 46.0 all-gather.14
  157.6 46.0 all-gather.12
  243.9 76.7 reduce-scatter.4
  322.9 77.2 reduce-scatter.2

commit v2 on v1

v2 whole, which is shorter than its diff:
```python
import functools

import jax
import jax.numpy as jnp
from jax import lax
from jax.experimental import pallas as pl
from jax.experimental.pallas import tpu as pltpu
from jax.sharding import PartitionSpec as P

LANES = 128
WIDTHS = (256, 128, 128)
SUBS = 8
MODES = 16
BLOCKS = 8
VMEM_BYTES = 60 * 1024 * 1024


def coefficients(residues, decay_rates, rows):
    return jnp.stack(
        [
            jnp.exp(-decay_rates),
            residues * jnp.sqrt(-jnp.expm1(-2.0 * decay_rates)),
            jnp.exp(-decay_rates * (rows // SUBS)),
            jnp.exp(-decay_rates * rows),
        ]
    )


def spread(coef_ref, which, lanes):
    table = coef_ref[which, :, lanes]
    return [jnp.broadcast_to(table[r : r + 1, :], (SUBS, LANES)) for r in range(MODES)]


def end_states(signal_ref, lanes, decay, run, backward):
    def step(j, state):
        at = run - 1 - j if backward else j
        row = signal_ref[pl.ds(at, SUBS, stride=run), lanes]
        return tuple(a * s + row for a, s in zip(decay, state))

    zero = jnp.zeros((SUBS, LANES), jnp.float32)
    return lax.fori_loop(0, run, step, (zero,) * MODES, unroll=8)


def full_scan(signal_ref, out_ref, decay, gain, state, run, backward):
    def step(j, state):
        at = run - 1 - j if backward else j
        rows = pl.ds(at, SUBS, stride=run)
        row = signal_ref[rows, :]
        state = tuple(a * s + row for a, s in zip(decay, state))
        terms = [g * s for g, s in zip(gain, state)]
        while len(terms) > 1:
            terms = [terms[i] + terms[i + 1] for i in range(0, len(terms), 2)]
        out_ref[rows, :] = terms[0]
        return state

    lax.fori_loop(0, run, step, tuple(state), unroll=8)


def branches_of(piece):
    return jnp.concatenate([piece[b] for b in range(3)], axis=1)


def bring(sources, targets, sems):
    copies = [pltpu.make_async_copy(a, b, sems.at[i]) for i, (a, b) in enumerate(zip(sources, targets))]
    for copy in copies:
        copy.start()
    return copies


def project_kernel(run, halves, order_ref, x_ref, *refs):
    count = sum(halves)
    pieces, (g_ref, coef_ref, proj_ref, runs_ref, ends_ref), refs = refs[:count], refs[count : count + 5], refs[count + 5 :]
    weights, (x, acc, mix, gmix, x_sems, w_sems) = refs[:count], refs[count:]
    width = g_ref.shape[1]
    depth = x_ref.shape[1] // len(halves)
    blocks = [x_ref.at[:, pl.ds(pl.multiple_of(order_ref[r] * depth, depth), depth)] for r in range(len(halves))]
    moves, parts_in = [], bring(pieces[:1], weights[:1], w_sems)
    moves = bring(blocks, [x.at[r] for r in range(len(halves))], x_sems)
    parts_in += bring(pieces[1:], weights[1:], w_sems.at[pl.ds(1, count - 1)])
    at = 0
    for r, parts in enumerate(halves):
        part = depth // parts
        moves[r].wait()
        for i in range(parts):
            parts_in[at].wait()
            left = x[r, :, i * part : (i + 1) * part]
            term = jnp.dot(left, branches_of(weights[at]), preferred_element_type=jnp.float32)
            if at:
                acc[...] += term
            else:
                acc[...] = term
            at += 1
    for b in range(3):
        proj_ref[b] = acc[:, b * width : (b + 1) * width].astype(jnp.bfloat16)
    for lane in range(0, width, LANES):
        lanes = slice(lane, lane + LANES)
        mix[...] = proj_ref[1, :, lanes].astype(jnp.float32) * proj_ref[2, :, lanes].astype(jnp.float32)
        gmix[...] = g_ref[:, lanes].astype(jnp.float32) * proj_ref[0, :, lanes].astype(jnp.float32)
        decay = spread(coef_ref, 0, lanes)
        long = coef_ref[2, :, lanes]
        for way, signal in enumerate((mix, gmix)):
            state = end_states(signal, slice(None), decay, run, way == 1)
            for r in range(MODES):
                runs_ref[way, lane // LANES, pl.ds(r, SUBS, stride=MODES), :] = state[r]
            total = jnp.zeros((MODES, LANES), jnp.float32)
            for i in range(SUBS):
                at = SUBS - 1 - i if way else i
                total = long * total + runs_ref[way, lane // LANES, at * MODES : (at + 1) * MODES, :]
            ends_ref[way, :, lanes] = total


def scan_kernel(run, place_ref, proj_ref, g_ref, coef_ref, skip_ref, runs_ref, ends_ref, gated_ref, gp_ref, mix, out, start):
    me = place_ref[0]
    count = ends_ref.shape[0]
    width = g_ref.shape[1]
    for lane in range(0, width, LANES):
        lanes = slice(lane, lane + LANES)
        decay = spread(coef_ref, 0, lanes)
        gain = spread(coef_ref, 1, lanes)
        long = coef_ref[2, :, lanes]
        whole = coef_ref[3, :, lanes]
        skip = skip_ref[:, lanes]
        grad = g_ref[:, lanes].astype(jnp.float32)
        query, key, value = [proj_ref[b, :, lanes].astype(jnp.float32) for b in range(3)]
        for way in range(2):
            state = jnp.zeros((MODES, LANES), jnp.float32)
            for i in range(count - 1):
                at = count - 1 - i if way else i
                keep = me < at if way else at < me
                state = jnp.where(keep, whole * state + ends_ref[at, way, :, lanes], state)
            for i in range(SUBS):
                at = SUBS - 1 - i if way else i
                start[at * MODES : (at + 1) * MODES, :] = state
                state = long * state + runs_ref[way, lane // LANES, at * MODES : (at + 1) * MODES, :]
            first = [start[pl.ds(r, SUBS, stride=MODES), :] for r in range(MODES)]
            mix[...] = grad * query if way else key * value
            full_scan(mix, out, decay, gain, first, run, way == 1)
            filtered = out[...] + skip * mix[...]
            if way:
                gp_ref[:, width + lane : width + lane + LANES] = (filtered * value).astype(jnp.bfloat16)
                gp_ref[:, 2 * width + lane : 2 * width + lane + LANES] = (filtered * key).astype(jnp.bfloat16)
            else:
                gated_ref[:, lanes] = (query * filtered).astype(jnp.bfloat16)
                gp_ref[:, lane : lane + LANES] = (grad * filtered).astype(jnp.bfloat16)


def at_rest(shape):
    return pl.BlockSpec(shape, lambda *_: (0,) * len(shape))


def away():
    return pl.BlockSpec(memory_space=pltpu.HBM)


def project(order, tokens, pieces, grad_out, coef):
    rows, inputs = tokens.shape
    width = grad_out.shape[1]
    flat = [part for piece in pieces for part in piece]
    groups = width // LANES
    return pl.pallas_call(
        functools.partial(project_kernel, rows // SUBS, [len(piece) for piece in pieces]),
        grid_spec=pltpu.PrefetchScalarGridSpec(
            num_scalar_prefetch=1,
            grid=(1,),
            in_specs=[away()] * (1 + len(flat)) + [at_rest(grad_out.shape), at_rest(coef.shape)],
            out_specs=[
                at_rest((3, rows, width)),
                at_rest((2, groups, SUBS * MODES, LANES)),
                at_rest((2, MODES, width)),
            ],
            scratch_shapes=[pltpu.VMEM(a.shape, a.dtype) for a in flat]
            + [
                pltpu.VMEM((len(pieces), rows, inputs // len(pieces)), tokens.dtype),
                pltpu.VMEM((rows, 3 * width), jnp.float32),
                pltpu.VMEM((rows, LANES), jnp.float32),
                pltpu.VMEM((rows, LANES), jnp.float32),
                pltpu.SemaphoreType.DMA((len(pieces),)),
                pltpu.SemaphoreType.DMA((len(flat),)),
            ],
        ),
        out_shape=[
            jax.ShapeDtypeStruct((3, rows, width), jnp.bfloat16),
            jax.ShapeDtypeStruct((2, groups, SUBS * MODES, LANES), jnp.float32),
            jax.ShapeDtypeStruct((2, MODES, width), jnp.float32),
        ],
        compiler_params=pltpu.CompilerParams(vmem_limit_bytes=VMEM_BYTES),
        cost_estimate=pl.CostEstimate(
            flops=2 * rows * inputs * 3 * width, bytes_accessed=2 * inputs * (rows + 3 * width), transcendentals=0
        ),
        name="project",
    )(order, tokens, *flat, grad_out, coef)


def scan(place, proj, grad_out, coef, skip, runs, ends):
    _, rows, width = proj.shape
    return pl.pallas_call(
        functools.partial(scan_kernel, rows // SUBS),
        grid_spec=pltpu.PrefetchScalarGridSpec(
            num_scalar_prefetch=1,
            grid=(1,),
            in_specs=[at_rest(a.shape) for a in (proj, grad_out, coef, skip, runs, ends)],
            out_specs=[at_rest((rows, width)), at_rest((rows, 3 * width))],
            scratch_shapes=[
                pltpu.VMEM((rows, LANES), jnp.float32),
                pltpu.VMEM((rows, LANES), jnp.float32),
                pltpu.VMEM((SUBS * MODES, LANES), jnp.float32),
            ],
        ),
        out_shape=[
            jax.ShapeDtypeStruct((rows, width), jnp.bfloat16),
            jax.ShapeDtypeStruct((rows, 3 * width), jnp.bfloat16),
        ],
        compiler_params=pltpu.CompilerParams(vmem_limit_bytes=VMEM_BYTES // 4),
        cost_estimate=pl.CostEstimate(flops=rows * width * MODES * 16, bytes_accessed=12 * rows * width, transcendentals=0),
        name="scan",
    )(place, proj, grad_out, coef, skip, runs, ends)


def input_grad_kernel(halves, core, pick_ref, *refs):
    chunks = len(halves)
    counts = [sum(h) for h in halves]
    places, total = [], 0
    for c in range(chunks):
        width = refs[c].shape[1] // 3
        places.append([slice(total + b * width, total + (b + 1) * width) for b in range(3)])
        total += 3 * width
    grads, refs = refs[:chunks], refs[chunks:]
    pieces, refs = refs[: sum(counts)], refs[sum(counts) :]
    out_ref, weights, sems = refs
    r_wanted = pick_ref[0]
    depth = weights.shape[0]
    at = 0
    for c, parts_of in enumerate(halves):
        for r, parts in enumerate(parts_of):

            @pl.when(r_wanted == r)
            def _(c=c, r=r, parts=parts, at=at):
                part = depth // parts
                for i in range(parts):
                    for b in range(3):
                        place = weights.at[i * part : (i + 1) * part, places[c][b]]
                        pltpu.make_async_copy(pieces[at + i].at[b], place, sems.at[c, b]).start()

            at += parts
    left = jnp.concatenate([g[...] for g in grads], axis=1)
    for c in range(chunks):
        for b in range(3):
            place = weights.at[:, places[c][b]]
            pltpu.make_async_copy(place, place, sems.at[c, b]).wait()
    total = lax.dot_general(left, weights[...], (((1,), (1,)), ((), ())), preferred_element_type=jnp.float32)
    out_ref[...] = total.astype(jnp.bfloat16)


def input_grad(pick, grads, weights, core):
    rows = grads[0].shape[0]
    depth = weights[0][0][0].shape[1]
    inner = sum(g.shape[1] for g in grads)
    halves = [[len(piece) for piece in pieces] for pieces in weights]
    flat = [part for pieces in weights for piece in pieces for part in piece]
    return pl.pallas_call(
        functools.partial(input_grad_kernel, halves, core),
        grid_spec=pltpu.PrefetchScalarGridSpec(
            num_scalar_prefetch=1,
            grid=(1,),
            in_specs=[at_rest(g.shape) for g in grads] + [away()] * len(flat),
            out_specs=at_rest((rows, depth)),
            scratch_shapes=[
                pltpu.VMEM((depth, inner), jnp.bfloat16),
                pltpu.SemaphoreType.DMA((len(grads), 3)),
            ],
        ),
        out_shape=jax.ShapeDtypeStruct((rows, depth), jnp.bfloat16),
        compiler_params=pltpu.CompilerParams(vmem_limit_bytes=VMEM_BYTES),
        cost_estimate=pl.CostEstimate(
            flops=2 * rows * depth * inner, bytes_accessed=2 * (inner * (rows + depth) + rows * depth), transcendentals=0
        ),
        name="input_grad",
    )(pick, *grads, *flat)


def exchange(array, axis, bit):
    count = lax.axis_size(axis)
    return lax.ppermute(array, axis, [(i, i ^ bit) for i in range(count)])


def after(value, *others):
    return lax.optimization_barrier((value, *others))[0]


class Plane:
    def __init__(self, blocks):
        self.held = []
        for c, mine in enumerate(blocks):
            if c == 1:
                mine = after(mine, self.held[0][0][0][1])
            elif c:
                mine = after(mine, self.held[c - 2][2][0][0], self.held[c - 2][4][0][0])
            far_x, far_y = exchange(mine, "seq", 2), exchange(mine, "seq", 4)
            self.held.append({0: [(mine, exchange(mine, "seq", 1))], 2: [(far_x,)], 4: [(far_y,)]})

    def relay(self, c, *gate):
        held = self.held[c]
        far_x, far_y = held[2][0][0], held[4][0][0]
        axis = far_x.ndim - 2
        half = far_x.shape[axis] // 2
        low = lax.slice_in_dim(far_x, 0, half, axis=axis)
        high = lax.slice_in_dim(far_y, half, 2 * half, axis=axis)
        gate += tuple(part[0] for part in self.held[c - 1][6]) if c else ()
        if gate:
            low, high = after((low, high), *gate)
        held[6] = [(exchange(low, "seq", 4),), (exchange(high, "seq", 2),)]

    def swap(self, c, *gate):
        for where in (2, 4, 6):
            blocks = [part[0] for part in self.held[c][where]]
            if gate:
                blocks = after(blocks, *gate)
            self.held[c][where] = [(part[0], exchange(block, "seq", 1)) for part, block in zip(self.held[c][where], blocks)]

    def pieces(self, c, places=(0, 2, 4, 6)):
        return [[pair[core] for pair in self.held[c][where]] for where in places for core in (0, 1)]


def gather_whole(mine):
    whole = lax.all_gather(mine, "seq", axis=1, tiled=True)
    return [[piece] for piece in jnp.split(whole, BLOCKS, axis=1)]


def local(tokens, proj_weight, residues, decay_rates, skip_gain, grad_out):
    rows = tokens.shape[0]
    depth = proj_weight.shape[0]
    channels = skip_gain.shape[0]
    groups = lax.axis_size("chan")
    me = lax.axis_index("seq").astype(jnp.int32)
    z = lax.axis_index("chan").astype(jnp.int32)
    direct = lax.axis_size("seq") == BLOCKS and groups == 4
    order = jnp.arange(BLOCKS, dtype=jnp.int32)
    if direct:
        order = order ^ me
    coef = coefficients(residues, decay_rates, rows)
    skip = skip_gain[None, :]
    branches = proj_weight.swapaxes(0, 1)
    slots, first = [], 0
    while first < channels:
        width = WIDTHS[min(len(slots), len(WIDTHS) - 1)]
        slots.append(slice(first, first + width))
        first += width
    chunks = len(slots)
    mine = [branches[:, :, lanes] for lanes in slots]

    def forward(c, pieces):
        lanes = slots[c]
        return project(order, tokens, pieces, grad_out[:, lanes], coef[:, :, lanes])

    def middle(span, made):
        ends = lax.all_gather(jnp.concatenate([m[2] for m in made], axis=2), "seq")
        gated, grads = [], []
        start = slots[span[0]].start
        for i, c in enumerate(span):
            lanes = slots[c]
            proj, runs, _ = made[i]
            seen = ends[:, :, :, lanes.start - start : lanes.stop - start]
            gate, grad = scan(me.reshape(1), proj, grad_out[:, lanes], coef[:, :, lanes], skip[:, lanes], runs, seen)
            gated.append(gate)
            grads.append(grad)
        return gated, grads

    if not direct:
        weights = [gather_whole(a) for a in mine]
        made = [forward(c, weights[c]) for c in range(chunks)]
        gated, grads = middle(range(chunks), made)
        flat = [jnp.concatenate([p[0][b] for p in pieces], axis=0) for pieces in weights for b in range(3)]
        contract = (((1,), (1,)), ((), ()))
        dx = lax.dot_general(jnp.concatenate(grads, axis=1), jnp.concatenate(flat, axis=1), contract, preferred_element_type=jnp.float32)
        grad_tokens = lax.psum_scatter(dx.astype(jnp.bfloat16), "chan", scatter_dimension=1, tiled=True)
        return (jnp.concatenate(gated, axis=1), grad_tokens)

    plane = Plane(mine)
    plane.relay(0)
    plane.swap(0)
    made = [forward(0, plane.pieces(0))]
    plane.relay(1)
    plane.swap(1, made[0][2])
    plane.relay(2, made[0][2])
    made.append(forward(1, plane.pieces(1)))
    plane.swap(2, made[1][2])
    made.append(forward(2, plane.pieces(2)))
    gated, grads = middle(range(chunks), made)
    weights = [plane.pieces(c) for c in range(chunks)]

    turns = jnp.array([[3, 2, 1, 0], [3, 2, 0, 1], [0, 1, 3, 2], [0, 1, 2, 3]], jnp.int32)[z]
    inwards, across, outwards = [(0, 1), (3, 2)], [(1, 2), (2, 1)], [(1, 0), (2, 3)]

    def part(turn, core):
        pick = me ^ (2 * turns[turn] + core)
        return input_grad(pick.reshape(1), grads, weights, core)

    def add(*terms):
        return sum(t.astype(jnp.float32) for t in terms).astype(jnp.bfloat16)

    sent = []

    def send(block, pairs):
        return lax.ppermute(block, "chan", pairs)

    parts = [[None, None] for _ in range(4)]
    got = [[None, None] for _ in range(3)]
    swapped = [[None, None] for _ in range(3)]
    for turn in range(3):
        for core in range(2):
            parts[turn][core] = part(turn, core)
            block = parts[turn][core]
            if len(sent) >= 2:
                block = after(block, sent[-2])
            got[turn][core] = send(block, inwards)
            sent.append(got[turn][core])
            if turn:
                swapped[turn][core] = send(add(parts[turn - 1][core], got[turn - 1][core]), across)
    out = []
    for core in range(2):
        last = part(3, core)
        back = send(add(parts[2][core], swapped[1][core]), outwards)
        out.append(add(last, got[2][core], swapped[2][core], back))
    return (jnp.concatenate(gated, axis=1), jnp.concatenate(out, axis=1))


def solution(mesh):
    placed = (
        P("seq", None),
        P("seq", None, "chan"),
        P(None, "chan"),
        P(None, "chan"),
        P("chan"),
        P("seq", "chan"),
    )
    return jax.shard_map(
        local,
        mesh=mesh,
        in_specs=placed,
        out_specs=(P("seq", "chan"), P("seq", "chan")),
        check_vma=False,
    )
```

time: 411 us -> 322 us (0.78)
  waiting for transfers between devices: 272 us -> 95.4 us
  starting transfers between devices: 0.24 us -> 66.7 us
  blocking collectives: 37.6 us -> 9.82 us
  other arithmetic: 3.99 us -> 25.1 us
  Pallas kernels: 73.9 us -> 95 us
  local copies, waits for them, and re-layouts: 7.63 us -> 24.5 us
  between operations: 14.3 us -> 3.77 us
    reduce_scatter x2 -> x0, waiting for transfers between devices: 144 us -> none  [local(): halves.append(lax.psum_scatter(dx, 'chan', scatter_dimension=1, tiled=True))]
    all_gather x4 -> x0, waiting for transfers between devices: 127 us -> none  [gather_chunk(): whole = lax.all_gather(part, 'seq')]
    ppermute x0 -> x39, waiting for transfers between devices: none -> 95.4 us  [the longest x27 66.5 us: exchange(): return lax.ppermute(array, axis, [(i, i ^ bit) for i in range(count)])]
    ppermute x0 -> x39, starting transfers between devices: none -> 66.7 us  [the longest x12 46.1 us: send(): return lax.ppermute(block, 'chan', pairs)]
    all_gather x4 -> x1, blocking collectives: 37.6 us -> 9.82 us  [middle(): ends = lax.all_gather(jnp.concatenate([m[2] for m in made], axis=2), 'seq')]
    pallas_call x10 -> x14, Pallas kernels: 73.9 us -> 95 us  [the longest x8 49.3 us: input_grad(): pl.pallas_call(functools.partial(input_grad_kernel, halves, core), grid_s...]
    convert_element_type x0 -> x8, other arithmetic: none -> 20.7 us  [add(): return sum((t.astype(jnp.float32) for t in terms)).astype(jnp.bfloat16)]
    slice x1 -> x16, local copies, waits for them, and re-layouts: 3.68 us -> 16.1 us  [the longest x3 4.75 us: relay(): high = lax.slice_in_dim(far_y, half, 2 * half, axis=axis)]
  transfers between devices with their start and end apart: 6 -> 39, of which waited for: 6 -> 11; matrix products, arithmetic and copies ran while one was open for 0% -> 11% of each run, Pallas kernels for 11% -> 22%
where the time goes in v2:
time: 322 us; the launch traced here: 320 us
  waiting for transfers between devices  95.4 us (30%)
  Pallas kernels  95 us (30%)
  starting transfers between devices  66.7 us (21%)
  other arithmetic  25.1 us (8%)
  local copies, waits for them, and re-layouts  24.5 us (8%)
  blocking collectives  9.82 us (3%)
  between operations  3.77 us (1%)
    ppermute x27, waiting for transfers between devices, exchange(): return lax.ppermute(array, axis, [(i, i ^ bit) for i in range(count)])  66.5 us
    pallas_call x8, Pallas kernels, input_grad(): pl.pallas_call(functools.partial(input_grad_kernel, halves, core), grid_s...  49.3 us
    ppermute x12, starting transfers between devices, send(): return lax.ppermute(block, 'chan', pairs)  46.1 us
    pallas_call x3, Pallas kernels, project(): pl.pallas_call(functools.partial(project_kernel, rows // SUBS, [len(piece...  37.6 us
    ppermute x12, waiting for transfers between devices, send(): return lax.ppermute(block, 'chan', pairs)  28.9 us
    convert_element_type x8, other arithmetic, add(): return sum((t.astype(jnp.float32) for t in terms)).astype(jnp.bfloat16)  20.7 us
    ppermute x27, starting transfers between devices, exchange(): return lax.ppermute(array, axis, [(i, i ^ bit) for i in range(count)])  20.6 us
    all_gather x1, blocking collectives, middle(): ends = lax.all_gather(jnp.concatenate([m[2] for m in made], axis=2), 'seq')  9.82 us
  transfers between devices with their start and end apart: 39, of which 11 were waited for; matrix products, arithmetic and copies ran while one was open for 11% of the time, Pallas kernels for 22%

profile of v2, /device:TPU:0, one launch (start us, length us, event | category | flops | bytes accessed | tf_op | source)
XLA Modules:
  0.0 320.2 jit_solution(17294035541977303179)
XLA Ops:
  0.6 1.7 slice.114.refs_0_.refs_3_
  2.8 2.6 collective-permute-start.1
  5.4 1.5 collective-permute-start.3
  7.3 1.5 collective-permute-start.10
  8.7 32.0 %collective-permute-done.1.refs_2_.refs_5_ = bf16[3,1024,256]{2,1,0:T(8,128)(2,1)} collective-permute-done((bf16[3,1024,256]{2,1,0:T(8,128)(2,1)S(1)}, bf16[3,1024,256]{2,1,0:T(8,128)(2,1)}, u32[]{:S(2)}, u32[]{:S(2)}) %collective-permute-start.1) | collective-permute-done | bytes 1572896 | tf_op jit(solution)/shard_map/ppermute | solution.py:283
  40.8 1.2 slice.115
  42.5 2.0 collective-permute-start.5
  44.5 1.2 slice.116
  45.7 1.6 collective-permute-start.6
  47.3 10.2 %collective-permute-done.10.refs_2_.refs_15_ = bf16[3,1024,128]{2,1,0:T(8,128)(2,1)S(1)} collective-permute-done((bf16[3,1024,128]{2,1,0:T(8,128)(2,1)S(1)}, bf16[3,1024,128]{2,1,0:T(8,128)(2,1)S(1)}, u32[]{:S(2)}, u32[]{:S(2)}) %collective-permute-start.10) | collective-permute-done | bytes 786464 | tf_op jit(solution)/shard_map/ppermute | solution.py:283
  58.4 2.0 collective-permute-start.12
  60.4 2.7 collective-permute-done.5.refs_6_.refs_9_
  63.0 11.2 %collective-permute-done.6.refs_7_.refs_10_ = bf16[3,512,256]{2,1,0:T(8,128)(2,1)} collective-permute-done((bf16[3,512,256]{2,1,0:T(8,128)(2,1)S(1)}, bf16[3,512,256]{2,1,0:T(8,128)(2,1)}, u32[]{:S(2)}, u32[]{:S(2)}) %collective-permute-start.6) | collective-permute-done | bytes 786464 | tf_op jit(solution)/shard_map/ppermute | solution.py:283
  74.2 1.7 slice.92.refs_10_.g_ref
  77.1 1.8 slice.120
  79.4 1.8 slice.121
  81.2 1.8 collective-permute-start.19
  82.9 1.5 collective-permute-start.21
  85.3 17.3 %project.3 = (bf16[3,512,256]{2,1,0:T(8,128)(2,1)}, f32[2,2,128,128]{3,2,1,0:T(8,128)}, f32[2,16,256]{2,1,0:T(8,128)}) custom-call(s32[8]{0:T(128)} %iota_xor_fusion.order_ref, bf16[512,8192]{1,0:T(8,128)(2,1)} %x_ref.5, bf16[3,1024,256]{2,1,0:T(8,128)(2,1)} %copy-done.15, bf16[3,1024,256]{2,1,0:T(8,128)(2,1)} %copy-done.16, ...), custom_call_target="tpu_custom_call" | custom-call | flops 6442450944 | bytes 20971520 | tf_op jit(solution)/shard_map/project/pallas_call | solution.py:160
  102.6 8.3 %collective-permute-done.14.refs_6_.refs_19_ = bf16[3,512,128]{2,1,0:T(8,128)(2,1)S(1)} collective-permute-done((bf16[3,512,128]{2,1,0:T(8,128)(2,1)}, bf16[3,512,128]{2,1,0:T(8,128)(2,1)S(1)}, u32[]{:S(2)}, u32[]{:S(2)}) %collective-permute-start.14) | collective-permute-done | bytes 393248 | tf_op jit(solution)/shard_map/ppermute | solution.py:283
  112.6 1.7 fusion.2
  114.3 1.8 slice.123
  116.0 1.8 slice.124
  117.9 1.5 collective-permute-start.23
  121.1 10.2 %project.4 = (bf16[3,512,128]{2,1,0:T(8,128)(2,1)}, f32[2,1,128,128]{3,2,1,0:T(8,128)}, f32[2,16,128]{2,1,0:T(8,128)}) custom-call(s32[8]{0:T(128)} %iota_xor_fusion.order_ref, bf16[512,8192]{1,0:T(8,128)(2,1)} %x_ref.5, bf16[3,1024,128]{2,1,0:T(8,128)(2,1)} %copy-done.18, bf16[3,1024,128]{2,1,0:T(8,128)(2,1)} %collective-permute-done.9.refs_1_.refs_14_, ...), custom_call_target="tpu_custom_call" | custom-call | flops 3221225472 | bytes 14680064 | tf_op jit(solution)/shard_map/project/pallas_call | solution.py:160
  134.5 1.1 collective-permute-done.25.refs_8_.refs_31_
  137.4 10.1 %project.5 = (bf16[3,512,128]{2,1,0:T(8,128)(2,1)}, f32[2,1,128,128]{3,2,1,0:T(8,128)}, f32[2,16,128]{2,1,0:T(8,128)}) custom-call(s32[8]{0:T(128)} %iota_xor_fusion.order_ref, bf16[512,8192]{1,0:T(8,128)(2,1)} %x_ref.5, bf16[3,1024,128]{2,1,0:T(8,128)(2,1)} %copy-done.19, bf16[3,1024,128]{2,1,0:T(8,128)(2,1)} %collective-permute-done.18.refs_1_.refs_24_, ...), custom_call_target="tpu_custom_call" | custom-call | flops 3221225472 | bytes 14680064 | tf_op jit(solution)/shard_map/project/pallas_call | solution.py:160
  148.5 9.8 %all-gather = f32[16,16,512]{2,1,0:T(8,128)S(1)} all-gather(f32[2,16,512]{2,1,0:T(8,128)S(1)} %pad_maximum_fusion.3), channel_id=2, replica_groups=mesh['seq'=8,'chan'=4] {'seq'}, dimensions={0}, use_global_device_ids=true | all-gather | bytes 589824 | tf_op jit(solution)/shard_map/all_gather | solution.py:356
  158.4 1.0 copy-done.8
  160.3 2.2 scan.5
  163.2 2.0 scan.4
  165.9 4.0 %scan.3 = (bf16[512,256]{1,0:T(8,128)(2,1)S(1)}, bf16[512,768]{1,0:T(8,128)(2,1)S(1)}) custom-call(s32[1]{0:T(128)} %bitcast.place_ref, bf16[3,512,256]{2,1,0:T(8,128)(2,1)S(1)} %copy-done.6, bf16[512,256]{1,0:T(8,128)(2,1)S(1)} %copy-done.5, f32[4,16,256]{2,1,0:T(8,128)S(1)} %copy-done.12, f32[1,256]{1,0:T(1,128)S(1)} %slice.118.skip_ref, ...), custom_call_target="tpu_custom_call" | custom-call | flops 33554432 | bytes 1572864 | tf_op jit(solution)/shard_map/scan/pallas_call | solution.py:196
  170.8 6.1 %input_grad.15 = bf16[512,1024]{1,0:T(8,128)(2,1)} custom-call(s32[1]{0:T(128)} %bitcast.19.pick_ref, bf16[512,768]{1,0:T(8,128)(2,1)} %copy-done, bf16[512,384]{1,0:T(8,128)(2,1)} %copy-done.2, bf16[512,384]{1,0:T(8,128)(2,1)} %copy-done.1, bf16[3,1024,256]{2,1,0:T(8,128)(2,1)} %copy-done.15, bf16[3,1024,256]{2,1,0:T(8,128)(2,1)} %copy-done.16, ...), custom_call_target="tpu_custom_call" | custom-call | flops 1610612736 | bytes 5767168 | tf_op jit(solution)/shard_map/input_grad/pallas_call | solution.py:260
  176.9 4.5 %collective-permute-start.33 = (bf16[512,1024]{1,0:T(8,128)(2,1)}, bf16[512,1024]{1,0:T(8,128)(2,1)}, u32[]{:S(2)}, u32[]{:S(2)}) collective-permute-start(bf16[512,1024]{1,0:T(8,128)(2,1)} %input_grad.15), channel_id=1, source_target_pairs={{0,1},{3,2},{4,5},{7,6},{8,9},{11,10},{12,13},{15,14},{16,17},{19,... | collective-permute-start | bytes 3145736 | tf_op jit(solution)/shard_map/ppermute | solution.py:404
  181.4 6.2 %input_grad.11 = bf16[512,1024]{1,0:T(8,128)(2,1)} custom-call(s32[1]{0:T(128)} %bitcast.15.pick_ref, bf16[512,768]{1,0:T(8,128)(2,1)} %copy-done, bf16[512,384]{1,0:T(8,128)(2,1)} %copy-done.2, bf16[512,384]{1,0:T(8,128)(2,1)} %copy-done.1, bf16[3,1024,256]{2,1,0:T(8,128)(2,1)} %copy-done.15, bf16[3,1024,256]{2,1,0:T(8,128)(2,1)} %copy-done.16, ...), custom_call_target="tpu_custom_call" | custom-call | flops 1610612736 | bytes 5767168 | tf_op jit(solution)/shard_map/input_grad/pallas_call | solution.py:260
  187.6 2.3 collective-permute-start.27
  189.9 14.4 %collective-permute-done.33 = bf16[512,1024]{1,0:T(8,128)(2,1)} collective-permute-done((bf16[512,1024]{1,0:T(8,128)(2,1)}, bf16[512,1024]{1,0:T(8,128)(2,1)}, u32[]{:S(2)}, u32[]{:S(2)}) %collective-permute-start.33) | collective-permute-done | bytes 1048608 | tf_op jit(solution)/shard_map/ppermute | solution.py:404
  204.2 1.6 add_convert_fusion.2
  205.8 1.6 collective-permute-start.37
  208.8 6.2 %input_grad.14 = bf16[512,1024]{1,0:T(8,128)(2,1)} custom-call(s32[1]{0:T(128)} %bitcast.18.pick_ref, bf16[512,768]{1,0:T(8,128)(2,1)} %copy-done, bf16[512,384]{1,0:T(8,128)(2,1)} %copy-done.2, bf16[512,384]{1,0:T(8,128)(2,1)} %copy-done.1, bf16[3,1024,256]{2,1,0:T(8,128)(2,1)} %copy-done.15, bf16[3,1024,256]{2,1,0:T(8,128)(2,1)} %copy-done.16, ...), custom_call_target="tpu_custom_call" | custom-call | flops 1610612736 | bytes 5767168 | tf_op jit(solution)/shard_map/input_grad/pallas_call | solution.py:260
  215.0 7.2 %collective-permute-start.34 = (bf16[512,1024]{1,0:T(8,128)(2,1)}, bf16[512,1024]{1,0:T(8,128)(2,1)}, u32[]{:S(2)}, u32[]{:S(2)}) collective-permute-start(bf16[512,1024]{1,0:T(8,128)(2,1)} %input_grad.14), channel_id=1, source_target_pairs={{0,1},{3,2},{4,5},{7,6},{8,9},{11,10},{12,13},{15,14},{16,17},{19,... | collective-permute-start | bytes 3145736 | tf_op jit(solution)/shard_map/ppermute | solution.py:404
  222.2 4.5 %collective-permute-done.27 = bf16[512,1024]{1,0:T(8,128)(2,1)} collective-permute-done((bf16[512,1024]{1,0:T(8,128)(2,1)}, bf16[512,1024]{1,0:T(8,128)(2,1)}, u32[]{:S(2)}, u32[]{:S(2)}) %collective-permute-start.27) | collective-permute-done | bytes 1048608 | tf_op jit(solution)/shard_map/ppermute | solution.py:404
  226.7 2.6 add_convert_fusion.6
  229.3 1.7 collective-permute-start.31
  231.0 6.1 %input_grad.13 = bf16[512,1024]{1,0:T(8,128)(2,1)} custom-call(s32[1]{0:T(128)} %bitcast.17.pick_ref, bf16[512,768]{1,0:T(8,128)(2,1)} %copy-done, bf16[512,384]{1,0:T(8,128)(2,1)} %copy-done.2, bf16[512,384]{1,0:T(8,128)(2,1)} %copy-done.1, bf16[3,1024,256]{2,1,0:T(8,128)(2,1)} %copy-done.15, bf16[3,1024,256]{2,1,0:T(8,128)(2,1)} %copy-done.16, ...), custom_call_target="tpu_custom_call" | custom-call | flops 1610612736 | bytes 5767168 | tf_op jit(solution)/shard_map/input_grad/pallas_call | solution.py:260
  237.1 6.2 %input_grad.10 = bf16[512,1024]{1,0:T(8,128)(2,1)} custom-call(s32[1]{0:T(128)} %bitcast.13.pick_ref, bf16[512,768]{1,0:T(8,128)(2,1)} %copy-done, bf16[512,384]{1,0:T(8,128)(2,1)} %copy-done.2, bf16[512,384]{1,0:T(8,128)(2,1)} %copy-done.1, bf16[3,1024,256]{2,1,0:T(8,128)(2,1)} %copy-done.15, bf16[3,1024,256]{2,1,0:T(8,128)(2,1)} %copy-done.16, ...), custom_call_target="tpu_custom_call" | custom-call | flops 1610612736 | bytes 5767168 | tf_op jit(solution)/shard_map/input_grad/pallas_call | solution.py:260
  243.3 7.2 %collective-permute-start.28 = (bf16[512,1024]{1,0:T(8,128)(2,1)}, bf16[512,1024]{1,0:T(8,128)(2,1)}, u32[]{:S(2)}, u32[]{:S(2)}) collective-permute-start(bf16[512,1024]{1,0:T(8,128)(2,1)} %input_grad.10), channel_id=1, source_target_pairs={{0,1},{3,2},{4,5},{7,6},{8,9},{11,10},{12,13},{15,14},{16,17},{19,... | collective-permute-start | bytes 3145736 | tf_op jit(solution)/shard_map/ppermute | solution.py:404
  250.6 2.6 add_convert_fusion.1
  253.2 1.5 collective-permute-start.38
  254.7 6.1 %input_grad.9 = bf16[512,1024]{1,0:T(8,128)(2,1)} custom-call(s32[1]{0:T(128)} %bitcast.11.pick_ref, bf16[512,768]{1,0:T(8,128)(2,1)} %copy-done, bf16[512,384]{1,0:T(8,128)(2,1)} %copy-done.2, bf16[512,384]{1,0:T(8,128)(2,1)} %copy-done.1, bf16[3,1024,256]{2,1,0:T(8,128)(2,1)} %copy-done.15, bf16[3,1024,256]{2,1,0:T(8,128)(2,1)} %copy-done.16, ...), custom_call_target="tpu_custom_call" | custom-call | flops 1610612736 | bytes 5767168 | tf_op jit(solution)/shard_map/input_grad/pallas_call | solution.py:260
  260.9 3.0 add_convert_fusion.3
  263.9 1.8 collective-permute-start.36
  265.7 6.9 %collective-permute-start.35 = (bf16[512,1024]{1,0:T(8,128)(2,1)S(1)}, bf16[512,1024]{1,0:T(8,128)(2,1)}, u32[]{:S(2)}, u32[]{:S(2)}) collective-permute-start(bf16[512,1024]{1,0:T(8,128)(2,1)S(1)} %copy-done.31), channel_id=1, source_target_pairs={{0,1},{3,2},{4,5},{7,6},{8,9},{11,10},{12,13},{15,14},{16,17},{19,... | collective-permute-start | bytes 3145736 | tf_op jit(solution)/shard_map/ppermute | solution.py:404
  272.6 2.6 add_convert_fusion.5
  275.2 1.3 collective-permute-start.32
  276.5 2.6 add_convert_fusion.7
  279.1 1.6 collective-permute-start.30
  280.8 8.4 %collective-permute-start.29 = (bf16[512,1024]{1,0:T(8,128)(2,1)S(1)}, bf16[512,1024]{1,0:T(8,128)(2,1)}, u32[]{:S(2)}, u32[]{:S(2)}) collective-permute-start(bf16[512,1024]{1,0:T(8,128)(2,1)S(1)} %copy-done.32), channel_id=1, source_target_pairs={{0,1},{3,2},{4,5},{7,6},{8,9},{11,10},{12,13},{15,14},{16,17},{19,... | collective-permute-start | bytes 3145736 | tf_op jit(solution)/shard_map/ppermute | solution.py:404
  290.6 6.1 %input_grad.12 = bf16[512,1024]{1,0:T(8,128)(2,1)} custom-call(s32[1]{0:T(128)} %bitcast.16.pick_ref, bf16[512,768]{1,0:T(8,128)(2,1)} %copy-done, bf16[512,384]{1,0:T(8,128)(2,1)} %copy-done.2, bf16[512,384]{1,0:T(8,128)(2,1)} %copy-done.1, bf16[3,1024,256]{2,1,0:T(8,128)(2,1)} %copy-done.15, bf16[3,1024,256]{2,1,0:T(8,128)(2,1)} %copy-done.16, ...), custom_call_target="tpu_custom_call" | custom-call | flops 1610612736 | bytes 5767168 | tf_op jit(solution)/shard_map/input_grad/pallas_call | solution.py:260
  296.7 6.3 %input_grad.8 = bf16[512,1024]{1,0:T(8,128)(2,1)} custom-call(s32[1]{0:T(128)} %bitcast.9.pick_ref, bf16[512,768]{1,0:T(8,128)(2,1)} %copy-done, bf16[512,384]{1,0:T(8,128)(2,1)} %copy-done.2, bf16[512,384]{1,0:T(8,128)(2,1)} %copy-done.1, bf16[3,1024,256]{2,1,0:T(8,128)(2,1)} %copy-done.15, bf16[3,1024,256]{2,1,0:T(8,128)(2,1)} %copy-done.16, ...), custom_call_target="tpu_custom_call" | custom-call | flops 1610612736 | bytes 5767168 | tf_op jit(solution)/shard_map/input_grad/pallas_call | solution.py:260
  303.0 2.8 add_convert_fusion
  305.9 10.1 %collective-permute-done.29 = bf16[512,1024]{1,0:T(8,128)(2,1)} collective-permute-done((bf16[512,1024]{1,0:T(8,128)(2,1)S(1)}, bf16[512,1024]{1,0:T(8,128)(2,1)}, u32[]{:S(2)}, u32[]{:S(2)}) %collective-permute-start.29) | collective-permute-done | bytes 1048608 | tf_op jit(solution)/shard_map/ppermute | solution.py:404
  315.9 2.8 add_convert_fusion.4
  318.7 1.5 pad_maximum_fusion
  (149 shorter events, 17.7 us)
Async XLA Ops:
  2.3 39.6 %copy-start.15 = (bf16[3,1024,256]{2,1,0:T(8,128)(2,1)}, bf16[3,1024,256]{2,1,0:T(8,128)(2,1)S(1)}, u32[]{:S(2)}) copy-start(bf16[3,1024,256]{2,1,0:T(8,128)(2,1)S(1)} %slice.114.refs_0_.refs_3_) | copy-start | bytes 4718596
  2.3 4.9 %collective-permute-start = (bf16[3,1024,256]{2,1,0:T(8,128)(2,1)S(1)}, bf16[3,1024,256]{2,1,0:T(8,128)(2,1)S(1)}, u32[]{:S(2)}, u32[]{:S(2)}) collective-permute-start(bf16[3,1024,256]{2,1,0:T(8,128)(2,1)S(1)} %slice.114.refs_0_.refs_3_), channel_id=1, source_target_pairs={{0,4},{4,0},{8,12},{12,8},{16,20},{20,16},{24,28},{28,24},{1,5},{5... | collective-permute-start | bytes 4718600 | tf_op jit(solution)/shard_map/ppermute | solution.py:283
  2.8 37.9 %collective-permute-start.1 = (bf16[3,1024,256]{2,1,0:T(8,128)(2,1)S(1)}, bf16[3,1024,256]{2,1,0:T(8,128)(2,1)}, u32[]{:S(2)}, u32[]{:S(2)}) collective-permute-start(bf16[3,1024,256]{2,1,0:T(8,128)(2,1)S(1)} %slice.114.refs_0_.refs_3_), channel_id=1, source_target_pairs={{0,8},{4,12},{8,0},{12,4},{16,24},{20,28},{24,16},{28,20},{1,9},{5... | collective-permute-start | bytes 4718600 | tf_op jit(solution)/shard_map/ppermute | solution.py:283
  5.4 36.6 %collective-permute-start.3 = (bf16[3,1024,256]{2,1,0:T(8,128)(2,1)S(1)}, bf16[3,1024,256]{2,1,0:T(8,128)(2,1)}, u32[]{:S(2)}, u32[]{:S(2)}) collective-permute-start(bf16[3,1024,256]{2,1,0:T(8,128)(2,1)S(1)} %slice.114.refs_0_.refs_3_), channel_id=1, source_target_pairs={{0,16},{4,20},{8,24},{12,28},{16,0},{20,4},{24,8},{28,12},{1,17},{... | collective-permute-start | bytes 4718600 | tf_op jit(solution)/shard_map/ppermute | solution.py:283
  7.2 95.4 %copy-start.18 = (bf16[3,1024,128]{2,1,0:T(8,128)(2,1)}, bf16[3,1024,128]{2,1,0:T(8,128)(2,1)S(1)}, u32[]{:S(2)}) copy-start(bf16[3,1024,128]{2,1,0:T(8,128)(2,1)S(1)} %get-tuple-element.38.refs_0_.refs_13_) | copy-start | bytes 2359300
  7.2 110.6 %copy-start.19 = (bf16[3,1024,128]{2,1,0:T(8,128)(2,1)}, bf16[3,1024,128]{2,1,0:T(8,128)(2,1)S(1)}, u32[]{:S(2)}) copy-start(bf16[3,1024,128]{2,1,0:T(8,128)(2,1)S(1)} %get-tuple-element.46.refs_0_.refs_23_) | copy-start | bytes 2359300
  7.2 68.7 %copy-start.39 = (f32[16,512]{1,0:T(8,128)S(1)}, f32[16,512]{1,0:T(8,128)}, u32[]{:S(2)}) copy-start(f32[16,512]{1,0:T(8,128)} %param.10) | copy-start | bytes 98308
  7.2 68.7 %copy-start.40 = (f32[16,512]{1,0:T(8,128)S(1)}, f32[16,512]{1,0:T(8,128)}, u32[]{:S(2)}) copy-start(f32[16,512]{1,0:T(8,128)} %param.9) | copy-start | bytes 98308
  7.2 34.7 %copy-start.16 = (bf16[3,1024,256]{2,1,0:T(8,128)(2,1)}, bf16[3,1024,256]{2,1,0:T(8,128)(2,1)S(1)}, u32[]{:S(2)}) copy-start(bf16[3,1024,256]{2,1,0:T(8,128)(2,1)S(1)} %collective-permute-done.refs_1_.refs_4_) | copy-start | bytes 4718596
  7.3 50.2 %collective-permute-start.10 = (bf16[3,1024,128]{2,1,0:T(8,128)(2,1)S(1)}, bf16[3,1024,128]{2,1,0:T(8,128)(2,1)S(1)}, u32[]{:S(2)}, u32[]{:S(2)}) collective-permute-start(bf16[3,1024,128]{2,1,0:T(8,128)(2,1)S(1)} %get-tuple-element.38.refs_0_.refs_13_), channel_id=1, source_target_pairs={{0,8},{4,12},{8,0},{12,4},{16,24},{20,28},{24,16},{28,20},{1,9},{5... | collective-permute-start | bytes 2359304 | tf_op jit(solution)/shard_map/ppermute | solution.py:283
  40.7 40.4 %collective-permute-start.2 = (bf16[3,1024,256]{2,1,0:T(8,128)(2,1)}, bf16[3,1024,256]{2,1,0:T(8,128)(2,1)}, u32[]{:S(2)}, u32[]{:S(2)}) collective-permute-start(bf16[3,1024,256]{2,1,0:T(8,128)(2,1)} %collective-permute-done.1.refs_2_.refs_5_), channel_id=1, source_target_pairs={{0,4},{4,0},{8,12},{12,8},{16,20},{20,16},{24,28},{28,24},{1,5},{5... | collective-permute-start | bytes 4718600 | tf_op jit(solution)/shard_map/ppermute | solution.py:283
  42.0 41.0 %collective-permute-start.4 = (bf16[3,1024,256]{2,1,0:T(8,128)(2,1)}, bf16[3,1024,256]{2,1,0:T(8,128)(2,1)S(1)}, u32[]{:S(2)}, u32[]{:S(2)}) collective-permute-start(bf16[3,1024,256]{2,1,0:T(8,128)(2,1)} %collective-permute-done.3.refs_4_.refs_7_), channel_id=1, source_target_pairs={{0,4},{4,0},{8,12},{12,8},{16,20},{20,16},{24,28},{28,24},{1,5},{5... | collective-permute-start | bytes 4718600 | tf_op jit(solution)/shard_map/ppermute | solution.py:283
  42.5 20.5 %collective-permute-start.5 = (bf16[3,512,256]{2,1,0:T(8,128)(2,1)S(1)}, bf16[3,512,256]{2,1,0:T(8,128)(2,1)}, u32[]{:S(2)}, u32[]{:S(2)}) collective-permute-start(bf16[3,512,256]{2,1,0:T(8,128)(2,1)S(1)} %slice.115), channel_id=1, source_target_pairs={{0,16},{4,20},{8,24},{12,28},{16,0},{20,4},{24,8},{28,12},{1,17},{... | collective-permute-start | bytes 2359304 | tf_op jit(solution)/shard_map/ppermute | solution.py:283
  45.7 28.5 %collective-permute-start.6 = (bf16[3,512,256]{2,1,0:T(8,128)(2,1)S(1)}, bf16[3,512,256]{2,1,0:T(8,128)(2,1)}, u32[]{:S(2)}, u32[]{:S(2)}) collective-permute-start(bf16[3,512,256]{2,1,0:T(8,128)(2,1)S(1)} %slice.116), channel_id=1, source_target_pairs={{0,8},{4,12},{8,0},{12,4},{16,24},{20,28},{24,16},{28,20},{1,9},{5... | collective-permute-start | bytes 2359304 | tf_op jit(solution)/shard_map/ppermute | solution.py:283
  58.4 20.9 %collective-permute-start.12 = (bf16[3,1024,128]{2,1,0:T(8,128)(2,1)S(1)}, bf16[3,1024,128]{2,1,0:T(8,128)(2,1)}, u32[]{:S(2)}, u32[]{:S(2)}) collective-permute-start(bf16[3,1024,128]{2,1,0:T(8,128)(2,1)S(1)} %get-tuple-element.38.refs_0_.refs_13_), channel_id=1, source_target_pairs={{0,16},{4,20},{8,24},{12,28},{16,0},{20,4},{24,8},{28,12},{1,17},{... | collective-permute-start | bytes 2359304 | tf_op jit(solution)/shard_map/ppermute | solution.py:283
  63.0 21.5 %collective-permute-start.7 = (bf16[3,512,256]{2,1,0:T(8,128)(2,1)}, bf16[3,512,256]{2,1,0:T(8,128)(2,1)}, u32[]{:S(2)}, u32[]{:S(2)}) collective-permute-start(bf16[3,512,256]{2,1,0:T(8,128)(2,1)} %collective-permute-done.5.refs_6_.refs_9_), channel_id=1, source_target_pairs={{0,4},{4,0},{8,12},{12,8},{16,20},{20,16},{24,28},{28,24},{1,5},{5... | collective-permute-start | bytes 2359304 | tf_op jit(solution)/shard_map/ppermute | solution.py:283
  74.2 10.8 %collective-permute-start.8 = (bf16[3,512,256]{2,1,0:T(8,128)(2,1)}, bf16[3,512,256]{2,1,0:T(8,128)(2,1)}, u32[]{:S(2)}, u32[]{:S(2)}) collective-permute-start(bf16[3,512,256]{2,1,0:T(8,128)(2,1)} %collective-permute-done.6.refs_7_.refs_10_), channel_id=1, source_target_pairs={{0,4},{4,0},{8,12},{12,8},{16,20},{20,16},{24,28},{28,24},{1,5},{5... | collective-permute-start | bytes 2359304 | tf_op jit(solution)/shard_map/ppermute | solution.py:283
  79.3 38.5 %collective-permute-start.9 = (bf16[3,1024,128]{2,1,0:T(8,128)(2,1)S(1)}, bf16[3,1024,128]{2,1,0:T(8,128)(2,1)}, u32[]{:S(2)}, u32[]{:S(2)}) collective-permute-start(bf16[3,1024,128]{2,1,0:T(8,128)(2,1)S(1)} %get-tuple-element.38.refs_0_.refs_13_), channel_id=1, source_target_pairs={{0,4},{4,0},{8,12},{12,8},{16,20},{20,16},{24,28},{28,24},{1,5},{5... | collective-permute-start | bytes 2359304 | tf_op jit(solution)/shard_map/ppermute | solution.py:283
  81.2 30.2 %collective-permute-start.19 = (bf16[3,1024,128]{2,1,0:T(8,128)(2,1)S(1)}, bf16[3,1024,128]{2,1,0:T(8,128)(2,1)}, u32[]{:S(2)}, u32[]{:S(2)}) collective-permute-start(bf16[3,1024,128]{2,1,0:T(8,128)(2,1)S(1)} %get-tuple-element.46.refs_0_.refs_23_), channel_id=1, source_target_pairs={{0,8},{4,12},{8,0},{12,4},{16,24},{20,28},{24,16},{28,20},{1,9},{5... | collective-permute-start | bytes 2359304 | tf_op jit(solution)/shard_map/ppermute | solution.py:283
  82.9 28.5 %collective-permute-start.21 = (bf16[3,1024,128]{2,1,0:T(8,128)(2,1)S(1)}, bf16[3,1024,128]{2,1,0:T(8,128)(2,1)}, u32[]{:S(2)}, u32[]{:S(2)}) collective-permute-start(bf16[3,1024,128]{2,1,0:T(8,128)(2,1)S(1)} %get-tuple-element.46.refs_0_.refs_23_), channel_id=1, source_target_pairs={{0,16},{4,20},{8,24},{12,28},{16,0},{20,4},{24,8},{28,12},{1,17},{... | collective-permute-start | bytes 2359304 | tf_op jit(solution)/shard_map/ppermute | solution.py:283
  84.5 26.4 %collective-permute-start.14 = (bf16[3,512,128]{2,1,0:T(8,128)(2,1)}, bf16[3,512,128]{2,1,0:T(8,128)(2,1)S(1)}, u32[]{:S(2)}, u32[]{:S(2)}) collective-permute-start(bf16[3,512,128]{2,1,0:T(8,128)(2,1)} %slice.120), channel_id=1, source_target_pairs={{0,16},{4,20},{8,24},{12,28},{16,0},{20,4},{24,8},{28,12},{1,17},{... | collective-permute-start | bytes 1179656 | tf_op jit(solution)/shard_map/ppermute | solution.py:283
  85.0 25.9 %collective-permute-start.15 = (bf16[3,512,128]{2,1,0:T(8,128)(2,1)}, bf16[3,512,128]{2,1,0:T(8,128)(2,1)S(1)}, u32[]{:S(2)}, u32[]{:S(2)}) collective-permute-start(bf16[3,512,128]{2,1,0:T(8,128)(2,1)} %slice.121), channel_id=1, source_target_pairs={{0,8},{4,12},{8,0},{12,4},{16,24},{20,28},{24,16},{28,20},{1,9},{5... | collective-permute-start | bytes 1179656 | tf_op jit(solution)/shard_map/ppermute | solution.py:283
  110.9 9.1 %collective-permute-start.11 = (bf16[3,1024,128]{2,1,0:T(8,128)(2,1)}, bf16[3,1024,128]{2,1,0:T(8,128)(2,1)S(1)}, u32[]{:S(2)}, u32[]{:S(2)}) collective-permute-start(bf16[3,1024,128]{2,1,0:T(8,128)(2,1)} %copy-done.20), channel_id=1, source_target_pairs={{0,4},{4,0},{8,12},{12,8},{16,20},{20,16},{24,28},{28,24},{1,5},{5... | collective-permute-start | bytes 2359304 | tf_op jit(solution)/shard_map/ppermute | solution.py:283
  110.9 9.1 %collective-permute-start.13 = (bf16[3,1024,128]{2,1,0:T(8,128)(2,1)}, bf16[3,1024,128]{2,1,0:T(8,128)(2,1)S(1)}, u32[]{:S(2)}, u32[]{:S(2)}) collective-permute-start(bf16[3,1024,128]{2,1,0:T(8,128)(2,1)} %collective-permute-done.12.refs_4_.refs_17_), channel_id=1, source_target_pairs={{0,4},{4,0},{8,12},{12,8},{16,20},{20,16},{24,28},{28,24},{1,5},{5... | collective-permute-start | bytes 2359304 | tf_op jit(solution)/shard_map/ppermute | solution.py:283
  111.4 6.5 %collective-permute-start.16 = (bf16[3,512,128]{2,1,0:T(8,128)(2,1)S(1)}, bf16[3,512,128]{2,1,0:T(8,128)(2,1)S(1)}, u32[]{:S(2)}, u32[]{:S(2)}) collective-permute-start(bf16[3,512,128]{2,1,0:T(8,128)(2,1)S(1)} %collective-permute-done.14.refs_6_.refs_19_), channel_id=1, source_target_pairs={{0,4},{4,0},{8,12},{12,8},{16,20},{20,16},{24,28},{28,24},{1,5},{5... | collective-permute-start | bytes 1179656 | tf_op jit(solution)/shard_map/ppermute | solution.py:283
  111.5 7.9 %collective-permute-start.17 = (bf16[3,512,128]{2,1,0:T(8,128)(2,1)S(1)}, bf16[3,512,128]{2,1,0:T(8,128)(2,1)S(1)}, u32[]{:S(2)}, u32[]{:S(2)}) collective-permute-start(bf16[3,512,128]{2,1,0:T(8,128)(2,1)S(1)} %collective-permute-done.15.refs_7_.refs_20_), channel_id=1, source_target_pairs={{0,4},{4,0},{8,12},{12,8},{16,20},{20,16},{24,28},{28,24},{1,5},{5... | collective-permute-start | bytes 1179656 | tf_op jit(solution)/shard_map/ppermute | solution.py:283
  117.8 16.7 %collective-permute-start.18 = (bf16[3,1024,128]{2,1,0:T(8,128)(2,1)S(1)}, bf16[3,1024,128]{2,1,0:T(8,128)(2,1)}, u32[]{:S(2)}, u32[]{:S(2)}) collective-permute-start(bf16[3,1024,128]{2,1,0:T(8,128)(2,1)S(1)} %get-tuple-element.46.refs_0_.refs_23_), channel_id=1, source_target_pairs={{0,4},{4,0},{8,12},{12,8},{16,20},{20,16},{24,28},{28,24},{1,5},{5... | collective-permute-start | bytes 2359304 | tf_op jit(solution)/shard_map/ppermute | solution.py:283
  117.9 14.0 %collective-permute-start.23 = (bf16[3,512,128]{2,1,0:T(8,128)(2,1)}, bf16[3,512,128]{2,1,0:T(8,128)(2,1)}, u32[]{:S(2)}, u32[]{:S(2)}) collective-permute-start(bf16[3,512,128]{2,1,0:T(8,128)(2,1)} %slice.123), channel_id=1, source_target_pairs={{0,16},{4,20},{8,24},{12,28},{16,0},{20,4},{24,8},{28,12},{1,17},{... | collective-permute-start | bytes 1179656 | tf_op jit(solution)/shard_map/ppermute | solution.py:283
  119.4 12.4 %collective-permute-start.24 = (bf16[3,512,128]{2,1,0:T(8,128)(2,1)}, bf16[3,512,128]{2,1,0:T(8,128)(2,1)}, u32[]{:S(2)}, u32[]{:S(2)}) collective-permute-start(bf16[3,512,128]{2,1,0:T(8,128)(2,1)} %slice.124), channel_id=1, source_target_pairs={{0,8},{4,12},{8,0},{12,4},{16,24},{20,28},{24,16},{28,20},{1,9},{5... | collective-permute-start | bytes 1179656 | tf_op jit(solution)/shard_map/ppermute | solution.py:283
  121.1 10.7 %copy-start.43 = (f32[512]{0:T(512)S(1)}, f32[512]{0:T(512)}, u32[]{:S(2)}) copy-start(f32[512]{0:T(512)} %param.11) | copy-start | bytes 6148
  131.3 4.8 %collective-permute-start.20 = (bf16[3,1024,128]{2,1,0:T(8,128)(2,1)}, bf16[3,1024,128]{2,1,0:T(8,128)(2,1)S(1)}, u32[]{:S(2)}, u32[]{:S(2)}) collective-permute-start(bf16[3,1024,128]{2,1,0:T(8,128)(2,1)} %collective-permute-done.19.refs_2_.refs_25_), channel_id=1, source_target_pairs={{0,4},{4,0},{8,12},{12,8},{16,20},{20,16},{24,28},{28,24},{1,5},{5... | collective-permute-start | bytes 2359304 | tf_op jit(solution)/shard_map/ppermute | solution.py:283
  131.4 4.7 %collective-permute-start.22 = (bf16[3,1024,128]{2,1,0:T(8,128)(2,1)}, bf16[3,1024,128]{2,1,0:T(8,128)(2,1)S(1)}, u32[]{:S(2)}, u32[]{:S(2)}) collective-permute-start(bf16[3,1024,128]{2,1,0:T(8,128)(2,1)} %collective-permute-done.21.refs_4_.refs_27_), channel_id=1, source_target_pairs={{0,4},{4,0},{8,12},{12,8},{16,20},{20,16},{24,28},{28,24},{1,5},{5... | collective-permute-start | bytes 2359304 | tf_op jit(solution)/shard_map/ppermute | solution.py:283
  131.9 3.7 %collective-permute-start.25 = (bf16[3,512,128]{2,1,0:T(8,128)(2,1)}, bf16[3,512,128]{2,1,0:T(8,128)(2,1)S(1)}, u32[]{:S(2)}, u32[]{:S(2)}) collective-permute-start(bf16[3,512,128]{2,1,0:T(8,128)(2,1)} %collective-permute-done.23.refs_6_.refs_29_), channel_id=1, source_target_pairs={{0,4},{4,0},{8,12},{12,8},{16,20},{20,16},{24,28},{28,24},{1,5},{5... | collective-permute-start | bytes 1179656 | tf_op jit(solution)/shard_map/ppermute | solution.py:283
  132.0 4.1 %collective-permute-start.26 = (bf16[3,512,128]{2,1,0:T(8,128)(2,1)}, bf16[3,512,128]{2,1,0:T(8,128)(2,1)S(1)}, u32[]{:S(2)}, u32[]{:S(2)}) collective-permute-start(bf16[3,512,128]{2,1,0:T(8,128)(2,1)} %collective-permute-done.24.refs_7_.refs_30_), channel_id=1, source_target_pairs={{0,4},{4,0},{8,12},{12,8},{16,20},{20,16},{24,28},{28,24},{1,5},{5... | collective-permute-start | bytes 1179656 | tf_op jit(solution)/shard_map/ppermute | solution.py:283
  137.4 10.2 %copy-start.41 = (f32[2,16,256]{2,1,0:T(8,128)S(1)}, f32[2,16,256]{2,1,0:T(8,128)}, u32[]{:S(2)}) copy-start(f32[2,16,256]{2,1,0:T(8,128)} %get-tuple-element.37) | copy-start | bytes 98308
  137.4 10.3 %copy-start.42 = (f32[2,16,128]{2,1,0:T(8,128)S(1)}, f32[2,16,128]{2,1,0:T(8,128)}, u32[]{:S(2)}) copy-start(f32[2,16,128]{2,1,0:T(8,128)} %get-tuple-element.45) | copy-start | bytes 49156
  137.4 21.0 %copy-start.4 = (bf16[512,128]{1,0:T(8,128)(2,1)S(1)}, bf16[512,128]{1,0:T(8,128)(2,1)}, u32[]{:S(2)}) copy-start(bf16[512,128]{1,0:T(8,128)(2,1)} %get-tuple-element.72.refs_10_.g_ref) | copy-start | bytes 393220
  137.4 21.0 %copy-start.10 = (f32[4,16,128]{2,1,0:T(8,128)S(1)}, f32[4,16,128]{2,1,0:T(8,128)}, u32[]{:S(2)}) copy-start(f32[4,16,128]{2,1,0:T(8,128)} %get-tuple-element.74.refs_11_.coef_ref) | copy-start | bytes 98308
  137.4 25.8 %copy-start.13 = (f32[2,1,128,128]{3,2,1,0:T(8,128)S(1)}, f32[2,1,128,128]{3,2,1,0:T(8,128)}, u32[]{:S(2)}) copy-start(f32[2,1,128,128]{3,2,1,0:T(8,128)} %get-tuple-element.56.runs_ref) | copy-start | bytes 393220
  137.4 28.5 %copy-start.11 = (f32[2,2,128,128]{3,2,1,0:T(8,128)S(1)}, f32[2,2,128,128]{3,2,1,0:T(8,128)}, u32[]{:S(2)}) copy-start(f32[2,2,128,128]{3,2,1,0:T(8,128)} %get-tuple-element.36.runs_ref) | copy-start | bytes 786436
  147.6 15.7 %copy-start.3 = (bf16[512,128]{1,0:T(8,128)(2,1)S(1)}, bf16[512,128]{1,0:T(8,128)(2,1)}, u32[]{:S(2)}) copy-start(bf16[512,128]{1,0:T(8,128)(2,1)} %get-tuple-element.73.refs_10_.g_ref) | copy-start | bytes 393220
  147.6 15.6 %copy-start.7 = (bf16[3,512,128]{2,1,0:T(8,128)(2,1)S(1)}, bf16[3,512,128]{2,1,0:T(8,128)(2,1)}, u32[]{:S(2)}) copy-start(bf16[3,512,128]{2,1,0:T(8,128)(2,1)} %get-tuple-element.55.proj_ref) | copy-start | bytes 1179652
  147.6 15.6 %copy-start.9 = (f32[4,16,128]{2,1,0:T(8,128)S(1)}, f32[4,16,128]{2,1,0:T(8,128)}, u32[]{:S(2)}) copy-start(f32[4,16,128]{2,1,0:T(8,128)} %get-tuple-element.75.refs_11_.coef_ref) | copy-start | bytes 98308
  147.6 18.4 %copy-start.5 = (bf16[512,256]{1,0:T(8,128)(2,1)S(1)}, bf16[512,256]{1,0:T(8,128)(2,1)}, u32[]{:S(2)}) copy-start(bf16[512,256]{1,0:T(8,128)(2,1)} %slice.92.refs_10_.g_ref) | copy-start | bytes 786436
  147.6 18.3 %copy-start.6 = (bf16[3,512,256]{2,1,0:T(8,128)(2,1)S(1)}, bf16[3,512,256]{2,1,0:T(8,128)(2,1)}, u32[]{:S(2)}) copy-start(bf16[3,512,256]{2,1,0:T(8,128)(2,1)} %get-tuple-element.35.proj_ref) | copy-start | bytes 2359300
  147.6 18.3 %copy-start.12 = (f32[4,16,256]{2,1,0:T(8,128)S(1)}, f32[4,16,256]{2,1,0:T(8,128)}, u32[]{:S(2)}) copy-start(f32[4,16,256]{2,1,0:T(8,128)} %slice.117.refs_11_.coef_ref) | copy-start | bytes 196612
  176.9 27.3 %collective-permute-start.33 = (bf16[512,1024]{1,0:T(8,128)(2,1)}, bf16[512,1024]{1,0:T(8,128)(2,1)}, u32[]{:S(2)}, u32[]{:S(2)}) collective-permute-start(bf16[512,1024]{1,0:T(8,128)(2,1)} %input_grad.15), channel_id=1, source_target_pairs={{0,1},{3,2},{4,5},{7,6},{8,9},{11,10},{12,13},{15,14},{16,17},{19,... | collective-permute-start | bytes 3145736 | tf_op jit(solution)/shard_map/ppermute | solution.py:404
  181.4 22.8 %copy-start.37 = (bf16[512,1024]{1,0:T(8,128)(2,1)S(1)}, bf16[512,1024]{1,0:T(8,128)(2,1)}, u32[]{:S(2)}) copy-start(bf16[512,1024]{1,0:T(8,128)(2,1)} %input_grad.15) | copy-start | bytes 3145732
  187.6 39.1 %collective-permute-start.27 = (bf16[512,1024]{1,0:T(8,128)(2,1)}, bf16[512,1024]{1,0:T(8,128)(2,1)}, u32[]{:S(2)}, u32[]{:S(2)}) collective-permute-start(bf16[512,1024]{1,0:T(8,128)(2,1)} %input_grad.11), channel_id=1, source_target_pairs={{0,1},{3,2},{4,5},{7,6},{8,9},{11,10},{12,13},{15,14},{16,17},{19,... | collective-permute-start | bytes 3145736 | tf_op jit(solution)/shard_map/ppermute | solution.py:404
  205.8 44.7 %collective-permute-start.37 = (bf16[512,1024]{1,0:T(8,128)(2,1)S(1)}, bf16[512,1024]{1,0:T(8,128)(2,1)}, u32[]{:S(2)}, u32[]{:S(2)}) collective-permute-start(bf16[512,1024]{1,0:T(8,128)(2,1)S(1)} %add_convert_fusion.2), channel_id=1, source_target_pairs={{1,2},{2,1},{5,6},{6,5},{9,10},{10,9},{13,14},{14,13},{17,18},{18,... | collective-permute-start | bytes 3145736 | tf_op jit(solution)/shard_map/ppermute | solution.py:404
  208.8 17.9 %copy-start.36 = (bf16[512,1024]{1,0:T(8,128)(2,1)S(1)}, bf16[512,1024]{1,0:T(8,128)(2,1)}, u32[]{:S(2)}) copy-start(bf16[512,1024]{1,0:T(8,128)(2,1)} %input_grad.11) | copy-start | bytes 3145732
  215.0 45.9 %collective-permute-start.34 = (bf16[512,1024]{1,0:T(8,128)(2,1)}, bf16[512,1024]{1,0:T(8,128)(2,1)}, u32[]{:S(2)}, u32[]{:S(2)}) collective-permute-start(bf16[512,1024]{1,0:T(8,128)(2,1)} %input_grad.14), channel_id=1, source_target_pairs={{0,1},{3,2},{4,5},{7,6},{8,9},{11,10},{12,13},{15,14},{16,17},{19,... | collective-permute-start | bytes 3145736 | tf_op jit(solution)/shard_map/ppermute | solution.py:404
  229.3 43.3 %collective-permute-start.31 = (bf16[512,1024]{1,0:T(8,128)(2,1)}, bf16[512,1024]{1,0:T(8,128)(2,1)}, u32[]{:S(2)}, u32[]{:S(2)}) collective-permute-start(bf16[512,1024]{1,0:T(8,128)(2,1)} %add_convert_fusion.6), channel_id=1, source_target_pairs={{1,2},{2,1},{5,6},{6,5},{9,10},{10,9},{13,14},{14,13},{17,18},{18,... | collective-permute-start | bytes 3145736 | tf_op jit(solution)/shard_map/ppermute | solution.py:404
  237.1 13.5 %copy-start.31 = (bf16[512,1024]{1,0:T(8,128)(2,1)S(1)}, bf16[512,1024]{1,0:T(8,128)(2,1)}, u32[]{:S(2)}) copy-start(bf16[512,1024]{1,0:T(8,128)(2,1)} %input_grad.13) | copy-start | bytes 3145732
  243.3 33.2 %collective-permute-start.28 = (bf16[512,1024]{1,0:T(8,128)(2,1)}, bf16[512,1024]{1,0:T(8,128)(2,1)}, u32[]{:S(2)}, u32[]{:S(2)}) collective-permute-start(bf16[512,1024]{1,0:T(8,128)(2,1)} %input_grad.10), channel_id=1, source_target_pairs={{0,1},{3,2},{4,5},{7,6},{8,9},{11,10},{12,13},{15,14},{16,17},{19,... | collective-permute-start | bytes 3145736 | tf_op jit(solution)/shard_map/ppermute | solution.py:404
  253.2 27.6 %collective-permute-start.38 = (bf16[512,1024]{1,0:T(8,128)(2,1)}, bf16[512,1024]{1,0:T(8,128)(2,1)}, u32[]{:S(2)}, u32[]{:S(2)}) collective-permute-start(bf16[512,1024]{1,0:T(8,128)(2,1)} %add_convert_fusion.1), channel_id=1, source_target_pairs={{1,0},{2,3},{5,4},{6,7},{9,8},{10,11},{13,12},{14,15},{17,16},{18,... | collective-permute-start | bytes 3145736 | tf_op jit(solution)/shard_map/ppermute | solution.py:404
  260.9 11.7 %copy-start.32 = (bf16[512,1024]{1,0:T(8,128)(2,1)S(1)}, bf16[512,1024]{1,0:T(8,128)(2,1)}, u32[]{:S(2)}) copy-start(bf16[512,1024]{1,0:T(8,128)(2,1)} %input_grad.9) | copy-start | bytes 3145732
  263.9 12.6 %copy-start.35 = (bf16[512,1024]{1,0:T(8,128)(2,1)S(1)}, bf16[512,1024]{1,0:T(8,128)(2,1)}, u32[]{:S(2)}) copy-start(bf16[512,1024]{1,0:T(8,128)(2,1)} %input_grad.10) | copy-start | bytes 3145732
  263.9 39.1 %collective-permute-start.36 = (bf16[512,1024]{1,0:T(8,128)(2,1)}, bf16[512,1024]{1,0:T(8,128)(2,1)}, u32[]{:S(2)}, u32[]{:S(2)}) collective-permute-start(bf16[512,1024]{1,0:T(8,128)(2,1)} %add_convert_fusion.3), channel_id=1, source_target_pairs={{1,2},{2,1},{5,6},{6,5},{9,10},{10,9},{13,14},{14,13},{17,18},{18,... | collective-permute-start | bytes 3145736 | tf_op jit(solution)/shard_map/ppermute | solution.py:404
  265.7 37.3 %collective-permute-start.35 = (bf16[512,1024]{1,0:T(8,128)(2,1)S(1)}, bf16[512,1024]{1,0:T(8,128)(2,1)}, u32[]{:S(2)}, u32[]{:S(2)}) collective-permute-start(bf16[512,1024]{1,0:T(8,128)(2,1)S(1)} %copy-done.31), channel_id=1, source_target_pairs={{0,1},{3,2},{4,5},{7,6},{8,9},{11,10},{12,13},{15,14},{16,17},{19,... | collective-permute-start | bytes 3145736 | tf_op jit(solution)/shard_map/ppermute | solution.py:404
  275.2 30.7 %collective-permute-start.32 = (bf16[512,1024]{1,0:T(8,128)(2,1)}, bf16[512,1024]{1,0:T(8,128)(2,1)}, u32[]{:S(2)}, u32[]{:S(2)}) collective-permute-start(bf16[512,1024]{1,0:T(8,128)(2,1)} %add_convert_fusion.5), channel_id=1, source_target_pairs={{1,0},{2,3},{5,4},{6,7},{9,8},{10,11},{13,12},{14,15},{17,16},{18,... | collective-permute-start | bytes 3145736 | tf_op jit(solution)/shard_map/ppermute | solution.py:404
  279.1 26.7 %collective-permute-start.30 = (bf16[512,1024]{1,0:T(8,128)(2,1)}, bf16[512,1024]{1,0:T(8,128)(2,1)}, u32[]{:S(2)}, u32[]{:S(2)}) collective-permute-start(bf16[512,1024]{1,0:T(8,128)(2,1)} %add_convert_fusion.7), channel_id=1, source_target_pairs={{1,2},{2,1},{5,6},{6,5},{9,10},{10,9},{13,14},{14,13},{17,18},{18,... | collective-permute-start | bytes 3145736 | tf_op jit(solution)/shard_map/ppermute | solution.py:404
  280.8 35.2 %collective-permute-start.29 = (bf16[512,1024]{1,0:T(8,128)(2,1)S(1)}, bf16[512,1024]{1,0:T(8,128)(2,1)}, u32[]{:S(2)}, u32[]{:S(2)}) collective-permute-start(bf16[512,1024]{1,0:T(8,128)(2,1)S(1)} %copy-done.32), channel_id=1, source_target_pairs={{0,1},{3,2},{4,5},{7,6},{8,9},{11,10},{12,13},{15,14},{16,17},{19,... | collective-permute-start | bytes 3145736 | tf_op jit(solution)/shard_map/ppermute | solution.py:404
  303.0 13.0 %copy-start.33 = (bf16[512,1024]{1,0:T(8,128)(2,1)S(1)}, bf16[512,1024]{1,0:T(8,128)(2,1)}, u32[]{:S(2)}) copy-start(bf16[512,1024]{1,0:T(8,128)(2,1)} %input_grad.8) | copy-start | bytes 3145732
  (19 other events, 47.3 us)

commit v3 on v2

--- a/solution.py
+++ b/solution.py
@@ -8,7 +8,7 @@
 from jax.sharding import PartitionSpec as P
 
 LANES = 128
-WIDTHS = (256, 128, 128)
+WIDTHS = (256, 256)
 SUBS = 8
 MODES = 16
 BLOCKS = 8
@@ -56,10 +56,6 @@
     lax.fori_loop(0, run, step, tuple(state), unroll=8)
 
 
-def branches_of(piece):
-    return jnp.concatenate([piece[b] for b in range(3)], axis=1)
-
-
 def bring(sources, targets, sems):
     copies = [pltpu.make_async_copy(a, b, sems.at[i]) for i, (a, b) in enumerate(zip(sources, targets))]
     for copy in copies:
@@ -67,31 +63,42 @@
     return copies
 
 
+def product(order_ref, x_ref, pieces, halves, x, w, x_sems, w_sems):
+    depth = x.shape[2]
+    width = w.shape[2] // 3
+    loads, at = [], 0
+    for r, parts in enumerate(halves):
+        columns = pl.ds(pl.multiple_of(order_ref[r] * depth, depth), depth)
+        load = bring([x_ref.at[:, columns]], [x.at[r]], x_sems.at[pl.ds(r, 1)])
+        part = depth // parts
+        for i in range(parts):
+            targets = [w.at[r, pl.ds(i * part, part), pl.ds(b * width, width)] for b in range(3)]
+            load += bring([pieces[at].at[b] for b in range(3)], targets, w_sems.at[at])
+            at += 1
+        loads.append(load)
+    total = None
+    for r in range(len(halves)):
+        for copy in loads[r]:
+            copy.wait()
+        term = jnp.dot(x[r], w[r], preferred_element_type=jnp.float32)
+        total = term if total is None else total + term
+    return total
+
+
+def project_part_kernel(halves, order_ref, x_ref, *refs):
+    count = sum(halves)
+    pieces, (out_ref, x, w, x_sems, w_sems) = refs[:count], refs[count:]
+    out_ref[...] = product(order_ref, x_ref, pieces, halves, x, w, x_sems, w_sems)
+
+
 def project_kernel(run, halves, order_ref, x_ref, *refs):
     count = sum(halves)
-    pieces, (g_ref, coef_ref, proj_ref, runs_ref, ends_ref), refs = refs[:count], refs[count : count + 5], refs[count + 5 :]
-    weights, (x, acc, mix, gmix, x_sems, w_sems) = refs[:count], refs[count:]
+    pieces, refs = refs[:count], refs[count:]
+    part_ref, g_ref, coef_ref, proj_ref, runs_ref, ends_ref, x, w, mix, gmix, x_sems, w_sems = refs
     width = g_ref.shape[1]
-    depth = x_ref.shape[1] // len(halves)
-    blocks = [x_ref.at[:, pl.ds(pl.multiple_of(order_ref[r] * depth, depth), depth)] for r in range(len(halves))]
-    moves, parts_in = [], bring(pieces[:1], weights[:1], w_sems)
-    moves = bring(blocks, [x.at[r] for r in range(len(halves))], x_sems)
-    parts_in += bring(pieces[1:], weights[1:], w_sems.at[pl.ds(1, count - 1)])
-    at = 0
-    for r, parts in enumerate(halves):
-        part = depth // parts
-        moves[r].wait()
-        for i in range(parts):
-            parts_in[at].wait()
-            left = x[r, :, i * part : (i + 1) * part]
-            term = jnp.dot(left, branches_of(weights[at]), preferred_element_type=jnp.float32)
-            if at:
-                acc[...] += term
-            else:
-                acc[...] = term
-            at += 1
+    total = part_ref[...] + product(order_ref, x_ref, pieces, halves, x, w, x_sems, w_sems)
     for b in range(3):
-        proj_ref[b] = acc[:, b * width : (b + 1) * width].astype(jnp.bfloat16)
+        proj_ref[b] = total[:, b * width : (b + 1) * width].astype(jnp.bfloat16)
     for lane in range(0, width, LANES):
         lanes = slice(lane, lane + LANES)
         mix[...] = proj_ref[1, :, lanes].astype(jnp.float32) * proj_ref[2, :, lanes].astype(jnp.float32)
@@ -152,31 +159,69 @@
     return pl.BlockSpec(memory_space=pltpu.HBM)
 
 
-def project(order, tokens, pieces, grad_out, coef):
+def block_scratch(tokens, pieces, width):
     rows, inputs = tokens.shape
+    depth = inputs // BLOCKS
+    parts = [len(piece) for piece in pieces]
+    buffers = [
+        pltpu.VMEM((len(pieces), rows, depth), tokens.dtype),
+        pltpu.VMEM((len(pieces), depth, 3 * width), tokens.dtype),
+    ]
+    return parts, buffers, [pltpu.SemaphoreType.DMA((len(pieces),)), pltpu.SemaphoreType.DMA((sum(parts), 3))]
+
+
+def product_cost(tokens, pieces, width):
+    rows = tokens.shape[0]
+    depth = tokens.shape[1] // BLOCKS * len(pieces)
+    return pl.CostEstimate(
+        flops=2 * rows * depth * 3 * width, bytes_accessed=2 * depth * (rows + 3 * width), transcendentals=0
+    )
+
+
+def project_part(order, tokens, pieces):
+    rows = tokens.shape[0]
+    flat = [part for piece in pieces for part in piece]
+    width = flat[0].shape[2]
+    halves, buffers, sems = block_scratch(tokens, pieces, width)
+    return pl.pallas_call(
+        functools.partial(project_part_kernel, halves),
+        grid_spec=pltpu.PrefetchScalarGridSpec(
+            num_scalar_prefetch=1,
+            grid=(1,),
+            in_specs=[away()] * (1 + len(flat)),
+            out_specs=at_rest((rows, 3 * width)),
+            scratch_shapes=buffers + sems,
+        ),
+        out_shape=jax.ShapeDtypeStruct((rows, 3 * width), jnp.float32),
+        compiler_params=pltpu.CompilerParams(vmem_limit_bytes=VMEM_BYTES),
+        cost_estimate=product_cost(tokens, pieces, width),
+        name="project_part",
+    )(order, tokens, *flat)
+
+
+def project(order, tokens, pieces, part, grad_out, coef):
+    rows = tokens.shape[0]
     width = grad_out.shape[1]
     flat = [part for piece in pieces for part in piece]
     groups = width // LANES
+    halves, buffers, sems = block_scratch(tokens, pieces, width)
     return pl.pallas_call(
-        functools.partial(project_kernel, rows // SUBS, [len(piece) for piece in pieces]),
+        functools.partial(project_kernel, rows // SUBS, halves),
         grid_spec=pltpu.PrefetchScalarGridSpec(
             num_scalar_prefetch=1,
             grid=(1,),
-            in_specs=[away()] * (1 + len(flat)) + [at_rest(grad_out.shape), at_rest(coef.shape)],
+            in_specs=[away()] * (1 + len(flat)) + [at_rest(a.shape) for a in (part, grad_out, coef)],
             out_specs=[
                 at_rest((3, rows, width)),
                 at_rest((2, groups, SUBS * MODES, LANES)),
                 at_rest((2, MODES, width)),
             ],
-            scratch_shapes=[pltpu.VMEM(a.shape, a.dtype) for a in flat]
+            scratch_shapes=buffers
             + [
-                pltpu.VMEM((len(pieces), rows, inputs // len(pieces)), tokens.dtype),
-                pltpu.VMEM((rows, 3 * width), jnp.float32),
                 pltpu.VMEM((rows, LANES), jnp.float32),
                 pltpu.VMEM((rows, LANES), jnp.float32),
-                pltpu.SemaphoreType.DMA((len(pieces),)),
-                pltpu.SemaphoreType.DMA((len(flat),)),
-            ],
+            ]
+            + sems,
         ),
         out_shape=[
             jax.ShapeDtypeStruct((3, rows, width), jnp.bfloat16),
@@ -184,11 +229,9 @@
             jax.ShapeDtypeStruct((2, MODES, width), jnp.float32),
         ],
         compiler_params=pltpu.CompilerParams(vmem_limit_bytes=VMEM_BYTES),
-        cost_estimate=pl.CostEstimate(
-            flops=2 * rows * inputs * 3 * width, bytes_accessed=2 * inputs * (rows + 3 * width), transcendentals=0
-        ),
+        cost_estimate=product_cost(tokens, pieces, width),
         name="project",
-    )(order, tokens, *flat, grad_out, coef)
+    )(order, tokens, *flat, part, grad_out, coef)
 
 
 def scan(place, proj, grad_out, coef, skip, runs, ends):
@@ -289,30 +332,34 @@
 
 class Plane:
     def __init__(self, blocks):
-        self.held = []
-        for c, mine in enumerate(blocks):
-            if c == 1:
-                mine = after(mine, self.held[0][0][0][1])
-            elif c:
-                mine = after(mine, self.held[c - 2][2][0][0], self.held[c - 2][4][0][0])
-            far_x, far_y = exchange(mine, "seq", 2), exchange(mine, "seq", 4)
-            self.held.append({0: [(mine, exchange(mine, "seq", 1))], 2: [(far_x,)], 4: [(far_y,)]})
+        self.blocks = blocks
+        self.held = [{} for _ in blocks]
+
+    def own(self, c, *gate):
+        mine = after(self.blocks[c], *gate) if gate else self.blocks[c]
+        self.held[c][2] = [(exchange(mine, "seq", 2),)]
+        self.held[c][4] = [(exchange(mine, "seq", 4),)]
+        self.held[c][0] = [(mine, exchange(mine, "seq", 1))]
+
+    def came(self, c, *places):
+        return [part[0] for where in places for part in self.held[c][where]]
+
+    def swapped(self, c, *places):
+        return [part[1] for where in places for part in self.held[c][where]]
 
     def relay(self, c, *gate):
-        held = self.held[c]
-        far_x, far_y = held[2][0][0], held[4][0][0]
+        far_x, far_y = self.came(c, 2, 4)
         axis = far_x.ndim - 2
         half = far_x.shape[axis] // 2
         low = lax.slice_in_dim(far_x, 0, half, axis=axis)
         high = lax.slice_in_dim(far_y, half, 2 * half, axis=axis)
-        gate += tuple(part[0] for part in self.held[c - 1][6]) if c else ()
         if gate:
             low, high = after((low, high), *gate)
-        held[6] = [(exchange(low, "seq", 4),), (exchange(high, "seq", 2),)]
-
-    def swap(self, c, *gate):
-        for where in (2, 4, 6):
-            blocks = [part[0] for part in self.held[c][where]]
+        self.held[c][6] = [(exchange(low, "seq", 4),), (exchange(high, "seq", 2),)]
+
+    def swap(self, c, places, *gate):
+        for where in places:
+            blocks = self.came(c, where)
             if gate:
                 blocks = after(blocks, *gate)
             self.held[c][where] = [(part[0], exchange(block, "seq", 1)) for part, block in zip(self.held[c][where], blocks)]
@@ -348,27 +395,33 @@
     chunks = len(slots)
     mine = [branches[:, :, lanes] for lanes in slots]
 
-    def forward(c, pieces):
+    def forward(c, pieces, part):
         lanes = slots[c]
-        return project(order, tokens, pieces, grad_out[:, lanes], coef[:, :, lanes])
-
-    def middle(span, made):
-        ends = lax.all_gather(jnp.concatenate([m[2] for m in made], axis=2), "seq")
+        count = len(pieces)
+        return project(order[BLOCKS - count :], tokens, pieces, part, grad_out[:, lanes], coef[:, :, lanes])
+
+    def meet(made):
+        return lax.all_gather(jnp.concatenate([m[2] for m in made], axis=2), "seq")
+
+    def scans(span, made, seen):
         gated, grads = [], []
         start = slots[span[0]].start
         for i, c in enumerate(span):
             lanes = slots[c]
             proj, runs, _ = made[i]
-            seen = ends[:, :, :, lanes.start - start : lanes.stop - start]
-            gate, grad = scan(me.reshape(1), proj, grad_out[:, lanes], coef[:, :, lanes], skip[:, lanes], runs, seen)
+            ends = seen[:, :, :, lanes.start - start : lanes.stop - start]
+            gate, grad = scan(me.reshape(1), proj, grad_out[:, lanes], coef[:, :, lanes], skip[:, lanes], runs, ends)
             gated.append(gate)
             grads.append(grad)
         return gated, grads
 
     if not direct:
         weights = [gather_whole(a) for a in mine]
-        made = [forward(c, weights[c]) for c in range(chunks)]
-        gated, grads = middle(range(chunks), made)
+        made = []
+        for c in range(chunks):
+            part = project_part(order[:6], tokens, weights[c][:6])
+            made.append(forward(c, weights[c][6:], part))
+        gated, grads = scans(range(chunks), made, meet(made))
         flat = [jnp.concatenate([p[0][b] for p in pieces], axis=0) for pieces in weights for b in range(3)]
         contract = (((1,), (1,)), ((), ()))
         dx = lax.dot_general(jnp.concatenate(grads, axis=1), jnp.concatenate(flat, axis=1), contract, preferred_element_type=jnp.float32)
@@ -376,16 +429,23 @@
         return (jnp.concatenate(gated, axis=1), grad_tokens)
 
     plane = Plane(mine)
+    near, far = (0, 2, 4), (6,)
+    plane.own(0)
     plane.relay(0)
-    plane.swap(0)
-    made = [forward(0, plane.pieces(0))]
-    plane.relay(1)
-    plane.swap(1, made[0][2])
-    plane.relay(2, made[0][2])
-    made.append(forward(1, plane.pieces(1)))
-    plane.swap(2, made[1][2])
-    made.append(forward(2, plane.pieces(2)))
-    gated, grads = middle(range(chunks), made)
+    plane.swap(0, (2, 4))
+    plane.own(1, *plane.swapped(0, 0, 2, 4))
+    plane.swap(0, far)
+    part = project_part(order[:6], tokens, plane.pieces(0, near))
+    made = [forward(0, plane.pieces(0, far), part)]
+    seen = meet(made)
+    plane.relay(1, seen)
+    plane.swap(1, (2, 4), seen)
+    gated, grads = scans((0,), made, seen)
+    part = project_part(order[:6], tokens, plane.pieces(1, near))
+    plane.swap(1, far, part, grads[0])
+    made.append(forward(1, plane.pieces(1, far), part))
+    late = scans((1,), made[1:], meet(made[1:]))
+    gated, grads = gated + late[0], grads + late[1]
     weights = [plane.pieces(c) for c in range(chunks)]
 
     turns = jnp.array([[3, 2, 1, 0], [3, 2, 0, 1], [0, 1, 3, 2], [0, 1, 2, 3]], jnp.int32)[z]

time: 322 us -> 311 us (0.966)
  waiting for transfers between devices: 95.4 us -> 82.8 us
  blocking collectives: 9.82 us -> 19.8 us
  starting transfers between devices: 66.7 us -> 58.5 us
  Pallas kernels: 95 us -> 102 us
  local copies, waits for them, and re-layouts: 24.5 us -> 18.8 us
    ppermute x27 -> x18, waiting for transfers between devices: 66.5 us -> 54.3 us  [exchange(): return lax.ppermute(array, axis, [(i, i ^ bit) for i in range(count)])]
    all_gather x1 -> x2, blocking collectives: 9.82 us -> 19.8 us  [meet(): return lax.all_gather(jnp.concatenate([m[2] for m in made], axis=2), 'seq')]
    ppermute x27 -> x18, starting transfers between devices: 20.6 us -> 12.3 us  [exchange(): return lax.ppermute(array, axis, [(i, i ^ bit) for i in range(count)])]
    pallas_call x3 -> x4, Pallas kernels: 37.6 us -> 44.9 us  [the longest x2 25.9 us: project_part(): pl.pallas_call(functools.partial(project_part_kernel, halves), grid_spec=...]
    unnamed x88 -> x50, local copies, waits for them, and re-layouts: 7.68 us -> 4.87 us
    pallas_call x3 -> x2, Pallas kernels: 8.09 us -> 7.91 us  [scan(): pl.pallas_call(functools.partial(scan_kernel, rows // SUBS), grid_spec=pl...]
  transfers between devices with their start and end apart: 39 -> 30, of which waited for: 11 -> 11; matrix products, arithmetic and copies ran while one was open for 11% -> 10% of each run, Pallas kernels for 22% -> 27%
where the time goes in v3:
time: 311 us; the launch traced here: 309 us
  Pallas kernels  102 us (33%)
  waiting for transfers between devices  82.8 us (27%)
  starting transfers between devices  58.5 us (19%)
  other arithmetic  23.5 us (8%)
  blocking collectives  19.8 us (6%)
  local copies, waits for them, and re-layouts  18.8 us (6%)
  between operations  3.51 us (1%)
    ppermute x18, waiting for transfers between devices, exchange(): return lax.ppermute(array, axis, [(i, i ^ bit) for i in range(count)])  54.3 us
    pallas_call x8, Pallas kernels, input_grad(): pl.pallas_call(functools.partial(input_grad_kernel, halves, core), grid_s...  49.3 us
    ppermute x12, starting transfers between devices, send(): return lax.ppermute(block, 'chan', pairs)  46.2 us
    ppermute x12, waiting for transfers between devices, send(): return lax.ppermute(block, 'chan', pairs)  28.5 us
    pallas_call x2, Pallas kernels, project_part(): pl.pallas_call(functools.partial(project_part_kernel, halves), grid_spec=...  25.9 us
    convert_element_type x8, other arithmetic, add(): return sum((t.astype(jnp.float32) for t in terms)).astype(jnp.bfloat16)  21.1 us
    all_gather x2, blocking collectives, meet(): return lax.all_gather(jnp.concatenate([m[2] for m in made], axis=2), 'seq')  19.8 us
    pallas_call x2, Pallas kernels, project(): pl.pallas_call(functools.partial(project_kernel, rows // SUBS, halves), g...  19 us
  transfers between devices with their start and end apart: 30, of which 11 were waited for; matrix products, arithmetic and copies ran while one was open for 10% of the time, Pallas kernels for 27%

profile of v3, /device:TPU:0, one launch (start us, length us, event | category | flops | bytes accessed | tf_op | source)
XLA Modules:
  0.0 309.0 jit_solution(10497975298909161165)
XLA Ops:
  0.6 2.1 fusion
  2.8 3.0 collective-permute-start
  5.8 1.5 collective-permute-start.2
  7.3 33.0 %collective-permute-done.refs_2_.refs_4_ = bf16[3,1024,256]{2,1,0:T(8,128)(2,1)} collective-permute-done((bf16[3,1024,256]{2,1,0:T(8,128)(2,1)S(1)}, bf16[3,1024,256]{2,1,0:T(8,128)(2,1)}, u32[]{:S(2)}, u32[]{:S(2)}) %collective-permute-start) | collective-permute-done | bytes 1572896 | tf_op jit(solution)/shard_map/ppermute | solution.py:326
  40.3 1.5 collective-permute-done.2.refs_4_.refs_6_
  41.7 2.1 slice.87
  43.8 1.5 collective-permute-start.1
  45.3 2.1 slice.88
  47.4 0.8 collective-permute-start.3
  48.2 1.3 collective-permute-start.9
  50.8 13.7 %collective-permute-done.1.refs_0_.refs_8_ = bf16[3,512,256]{2,1,0:T(8,128)(2,1)} collective-permute-done((bf16[3,512,256]{2,1,0:T(8,128)(2,1)}, bf16[3,512,256]{2,1,0:T(8,128)(2,1)}, u32[]{:S(2)}, u32[]{:S(2)}) %collective-permute-start.1) | collective-permute-done | bytes 786464 | tf_op jit(solution)/shard_map/ppermute | solution.py:326
  64.5 3.7 %collective-permute-done.3.refs_1_.refs_9_ = bf16[3,512,256]{2,1,0:T(8,128)(2,1)} collective-permute-done((bf16[3,512,256]{2,1,0:T(8,128)(2,1)}, bf16[3,512,256]{2,1,0:T(8,128)(2,1)}, u32[]{:S(2)}, u32[]{:S(2)}) %collective-permute-start.3) | collective-permute-done | bytes 786464 | tf_op jit(solution)/shard_map/ppermute | solution.py:326
  68.8 1.9 fusion.1
  71.1 13.0 %project_part.2.refs_4_ = f32[512,768]{1,0:T(8,128)} custom-call(s32[6]{0:T(128)} %bitcast.29, bf16[512,8192]{1,0:T(8,128)(2,1)} %x_ref.7, bf16[3,1024,256]{2,1,0:T(8,128)(2,1)} %copy-done.10, bf16[3,1024,256]{2,1,0:T(8,128)(2,1)} %collective-permute-done.6.refs_1_.refs_3_, bf16[3,1024,256]{2,1,0:T(8,128)(2,1)} %collective-permute-done.refs_2_.refs_4_, ...), custom_call_target="tpu_custom_call" | custom-call | flops 4831838208 | bytes 15728640 | tf_op jit(solution)/shard_map/project_part/pallas_call | solution.py:186
  84.1 9.4 %project.2 = (bf16[3,512,256]{2,1,0:T(8,128)(2,1)}, f32[2,2,128,128]{3,2,1,0:T(8,128)}, f32[2,16,256]{2,1,0:T(8,128)}) custom-call(s32[2]{0:T(128)} %slice.68.order_ref, bf16[512,8192]{1,0:T(8,128)(2,1)} %x_ref.7, bf16[3,512,256]{2,1,0:T(8,128)(2,1)} %collective-permute-done.1.refs_0_.refs_8_, bf16[3,512,256]{2,1,0:T(8,128)(2,1)} %collective-permute-done.3.refs_1_.refs_9_, ...), custom_call_target="tpu_custom_call" | custom-call | flops 1610612736 | bytes 5242880 | tf_op jit(solution)/shard_map/project/pallas_call | solution.py:208
  93.6 11.0 %all-gather = f32[16,16,256]{2,1,0:T(8,128)S(1)} all-gather(f32[2,16,256]{2,1,0:T(8,128)} %get-tuple-element.25), channel_id=2, replica_groups=mesh['seq'=8,'chan'=4] {'seq'}, dimensions={0}, use_global_device_ids=true | all-gather | bytes 294912 | tf_op jit(solution)/shard_map/all_gather | solution.py:404
  105.2 2.1 slice.92
  107.2 1.2 slice.93
  108.4 1.6 collective-permute-start.11
  110.5 4.0 %scan.2 = (bf16[512,256]{1,0:T(8,128)(2,1)S(1)}, bf16[512,768]{1,0:T(8,128)(2,1)S(1)}) custom-call(s32[1]{0:T(128)} %bitcast.place_ref, bf16[3,512,256]{2,1,0:T(8,128)(2,1)S(1)} %copy-done.4, bf16[512,256]{1,0:T(8,128)(2,1)S(1)} %copy-done.3, f32[4,16,256]{2,1,0:T(8,128)S(1)} %copy-done.7, f32[1,256]{1,0:T(1,128)S(1)} %get-tuple-element.55.skip_ref, ...), custom_call_target="tpu_custom_call" | custom-call | flops 33554432 | bytes 1572864 | tf_op jit(solution)/shard_map/scan/pallas_call | solution.py:239
  114.5 0.9 copy-done
  115.4 12.9 %project_part.3.refs_4_ = f32[512,768]{1,0:T(8,128)} custom-call(s32[6]{0:T(128)} %bitcast.30, bf16[512,8192]{1,0:T(8,128)(2,1)} %x_ref.7, bf16[3,1024,256]{2,1,0:T(8,128)(2,1)} %copy-done.11, bf16[3,1024,256]{2,1,0:T(8,128)(2,1)} %collective-permute-done.13.refs_1_.refs_13_, bf16[3,1024,256]{2,1,0:T(8,128)(2,1)} %collective-permute-done.9.refs_2_.refs_14_, ...), custom_call_target="tpu_custom_call" | custom-call | flops 4831838208 | bytes 15728640 | tf_op jit(solution)/shard_map/project_part/pallas_call | solution.py:186
  128.6 1.1 collective-permute-done.12.refs_1_.refs_19_
  130.2 0.7 constant_dynamic-slice_fusion
  132.1 1.0 collective-permute-done.16.refs_2_.refs_20_
  134.2 9.6 %project.3 = (bf16[3,512,256]{2,1,0:T(8,128)(2,1)}, f32[2,2,128,128]{3,2,1,0:T(8,128)}, f32[2,16,256]{2,1,0:T(8,128)}) custom-call(s32[2]{0:T(128)} %slice.68.order_ref, bf16[512,8192]{1,0:T(8,128)(2,1)} %x_ref.7, bf16[3,512,256]{2,1,0:T(8,128)(2,1)} %copy-done.12, bf16[3,512,256]{2,1,0:T(8,128)(2,1)} %collective-permute-done.12.refs_1_.refs_19_, ...), custom_call_target="tpu_custom_call" | custom-call | flops 1610612736 | bytes 5242880 | tf_op jit(solution)/shard_map/project/pallas_call | solution.py:208
  143.8 8.8 %all-gather.1 = f32[16,16,256]{2,1,0:T(8,128)S(1)} all-gather(f32[2,16,256]{2,1,0:T(8,128)} %get-tuple-element.37), channel_id=3, replica_groups=mesh['seq'=8,'chan'=4] {'seq'}, dimensions={0}, use_global_device_ids=true | all-gather | bytes 294912 | tf_op jit(solution)/shard_map/all_gather | solution.py:404
  152.5 1.1 copy-done.5
  153.7 0.9 copy-done.9
  154.6 4.0 %scan.3 = (bf16[512,256]{1,0:T(8,128)(2,1)S(1)}, bf16[512,768]{1,0:T(8,128)(2,1)S(1)}) custom-call(s32[1]{0:T(128)} %bitcast.place_ref, bf16[3,512,256]{2,1,0:T(8,128)(2,1)S(1)} %copy-done.5, bf16[512,256]{1,0:T(8,128)(2,1)S(1)} %copy-done.2, f32[4,16,256]{2,1,0:T(8,128)S(1)} %copy-done.6, f32[1,256]{1,0:T(1,128)S(1)} %get-tuple-element.54.skip_ref, ...), custom_call_target="tpu_custom_call" | custom-call | flops 33554432 | bytes 1572864 | tf_op jit(solution)/shard_map/scan/pallas_call | solution.py:239
  158.6 0.9 copy-done.1
  159.5 6.2 %input_grad.15 = bf16[512,1024]{1,0:T(8,128)(2,1)} custom-call(s32[1]{0:T(128)} %bitcast.20.pick_ref, bf16[512,768]{1,0:T(8,128)(2,1)} %copy-done, bf16[512,768]{1,0:T(8,128)(2,1)} %copy-done.1, bf16[3,1024,256]{2,1,0:T(8,128)(2,1)} %copy-done.10, bf16[3,1024,256]{2,1,0:T(8,128)(2,1)} %collective-permute-done.6.refs_1_.refs_3_, ...), custom_call_target="tpu_custom_call" | custom-call | flops 1610612736 | bytes 5767168 | tf_op jit(solution)/shard_map/input_grad/pallas_call | solution.py:303
  165.7 4.5 %collective-permute-start.24 = (bf16[512,1024]{1,0:T(8,128)(2,1)}, bf16[512,1024]{1,0:T(8,128)(2,1)}, u32[]{:S(2)}, u32[]{:S(2)}) collective-permute-start(bf16[512,1024]{1,0:T(8,128)(2,1)} %input_grad.15), channel_id=1, source_target_pairs={{0,1},{3,2},{4,5},{7,6},{8,9},{11,10},{12,13},{15,14},{16,17},{19,... | collective-permute-start | bytes 3145736 | tf_op jit(solution)/shard_map/ppermute | solution.py:464
  170.2 6.2 %input_grad.11 = bf16[512,1024]{1,0:T(8,128)(2,1)} custom-call(s32[1]{0:T(128)} %bitcast.16.pick_ref, bf16[512,768]{1,0:T(8,128)(2,1)} %copy-done, bf16[512,768]{1,0:T(8,128)(2,1)} %copy-done.1, bf16[3,1024,256]{2,1,0:T(8,128)(2,1)} %copy-done.10, bf16[3,1024,256]{2,1,0:T(8,128)(2,1)} %collective-permute-done.6.refs_1_.refs_3_, ...), custom_call_target="tpu_custom_call" | custom-call | flops 1610612736 | bytes 5767168 | tf_op jit(solution)/shard_map/input_grad/pallas_call | solution.py:303
  176.4 2.3 collective-permute-start.18
  178.6 14.3 %collective-permute-done.24 = bf16[512,1024]{1,0:T(8,128)(2,1)} collective-permute-done((bf16[512,1024]{1,0:T(8,128)(2,1)}, bf16[512,1024]{1,0:T(8,128)(2,1)}, u32[]{:S(2)}, u32[]{:S(2)}) %collective-permute-start.24) | collective-permute-done | bytes 1048608 | tf_op jit(solution)/shard_map/ppermute | solution.py:464
  193.0 1.6 add_convert_fusion.2
  194.6 1.6 collective-permute-start.28
  197.5 6.2 %input_grad.14 = bf16[512,1024]{1,0:T(8,128)(2,1)} custom-call(s32[1]{0:T(128)} %bitcast.19.pick_ref, bf16[512,768]{1,0:T(8,128)(2,1)} %copy-done, bf16[512,768]{1,0:T(8,128)(2,1)} %copy-done.1, bf16[3,1024,256]{2,1,0:T(8,128)(2,1)} %copy-done.10, bf16[3,1024,256]{2,1,0:T(8,128)(2,1)} %collective-permute-done.6.refs_1_.refs_3_, ...), custom_call_target="tpu_custom_call" | custom-call | flops 1610612736 | bytes 5767168 | tf_op jit(solution)/shard_map/input_grad/pallas_call | solution.py:303
  203.7 7.3 %collective-permute-start.25 = (bf16[512,1024]{1,0:T(8,128)(2,1)}, bf16[512,1024]{1,0:T(8,128)(2,1)}, u32[]{:S(2)}, u32[]{:S(2)}) collective-permute-start(bf16[512,1024]{1,0:T(8,128)(2,1)} %input_grad.14), channel_id=1, source_target_pairs={{0,1},{3,2},{4,5},{7,6},{8,9},{11,10},{12,13},{15,14},{16,17},{19,... | collective-permute-start | bytes 3145736 | tf_op jit(solution)/shard_map/ppermute | solution.py:464
  211.0 4.4 %collective-permute-done.18 = bf16[512,1024]{1,0:T(8,128)(2,1)} collective-permute-done((bf16[512,1024]{1,0:T(8,128)(2,1)}, bf16[512,1024]{1,0:T(8,128)(2,1)}, u32[]{:S(2)}, u32[]{:S(2)}) %collective-permute-start.18) | collective-permute-done | bytes 1048608 | tf_op jit(solution)/shard_map/ppermute | solution.py:464
  215.4 2.6 add_convert_fusion.6
  218.1 1.7 collective-permute-start.22
  219.7 6.1 %input_grad.13 = bf16[512,1024]{1,0:T(8,128)(2,1)} custom-call(s32[1]{0:T(128)} %bitcast.18.pick_ref, bf16[512,768]{1,0:T(8,128)(2,1)} %copy-done, bf16[512,768]{1,0:T(8,128)(2,1)} %copy-done.1, bf16[3,1024,256]{2,1,0:T(8,128)(2,1)} %copy-done.10, bf16[3,1024,256]{2,1,0:T(8,128)(2,1)} %collective-permute-done.6.refs_1_.refs_3_, ...), custom_call_target="tpu_custom_call" | custom-call | flops 1610612736 | bytes 5767168 | tf_op jit(solution)/shard_map/input_grad/pallas_call | solution.py:303
  225.9 6.2 %input_grad.10 = bf16[512,1024]{1,0:T(8,128)(2,1)} custom-call(s32[1]{0:T(128)} %bitcast.14.pick_ref, bf16[512,768]{1,0:T(8,128)(2,1)} %copy-done, bf16[512,768]{1,0:T(8,128)(2,1)} %copy-done.1, bf16[3,1024,256]{2,1,0:T(8,128)(2,1)} %copy-done.10, bf16[3,1024,256]{2,1,0:T(8,128)(2,1)} %collective-permute-done.6.refs_1_.refs_3_, ...), custom_call_target="tpu_custom_call" | custom-call | flops 1610612736 | bytes 5767168 | tf_op jit(solution)/shard_map/input_grad/pallas_call | solution.py:303
  232.1 7.2 %collective-permute-start.19 = (bf16[512,1024]{1,0:T(8,128)(2,1)}, bf16[512,1024]{1,0:T(8,128)(2,1)}, u32[]{:S(2)}, u32[]{:S(2)}) collective-permute-start(bf16[512,1024]{1,0:T(8,128)(2,1)} %input_grad.10), channel_id=1, source_target_pairs={{0,1},{3,2},{4,5},{7,6},{8,9},{11,10},{12,13},{15,14},{16,17},{19,... | collective-permute-start | bytes 3145736 | tf_op jit(solution)/shard_map/ppermute | solution.py:464
  239.3 2.7 add_convert_fusion.1
  241.9 1.3 collective-permute-start.29
  243.2 6.1 %input_grad.9 = bf16[512,1024]{1,0:T(8,128)(2,1)} custom-call(s32[1]{0:T(128)} %bitcast.12.pick_ref, bf16[512,768]{1,0:T(8,128)(2,1)} %copy-done, bf16[512,768]{1,0:T(8,128)(2,1)} %copy-done.1, bf16[3,1024,256]{2,1,0:T(8,128)(2,1)} %copy-done.10, bf16[3,1024,256]{2,1,0:T(8,128)(2,1)} %collective-permute-done.6.refs_1_.refs_3_, ...), custom_call_target="tpu_custom_call" | custom-call | flops 1610612736 | bytes 5767168 | tf_op jit(solution)/shard_map/input_grad/pallas_call | solution.py:303
  249.4 3.0 add_convert_fusion.3
  252.4 1.8 collective-permute-start.27
  254.2 7.2 %collective-permute-start.26 = (bf16[512,1024]{1,0:T(8,128)(2,1)S(1)}, bf16[512,1024]{1,0:T(8,128)(2,1)}, u32[]{:S(2)}, u32[]{:S(2)}) collective-permute-start(bf16[512,1024]{1,0:T(8,128)(2,1)S(1)} %copy-done.15), channel_id=1, source_target_pairs={{0,1},{3,2},{4,5},{7,6},{8,9},{11,10},{12,13},{15,14},{16,17},{19,... | collective-permute-start | bytes 3145736 | tf_op jit(solution)/shard_map/ppermute | solution.py:464
  261.4 2.6 add_convert_fusion.5
  264.0 1.3 collective-permute-start.23
  265.3 2.7 add_convert_fusion.7
  268.0 1.6 collective-permute-start.21
  269.6 8.5 %collective-permute-start.20 = (bf16[512,1024]{1,0:T(8,128)(2,1)S(1)}, bf16[512,1024]{1,0:T(8,128)(2,1)}, u32[]{:S(2)}, u32[]{:S(2)}) collective-permute-start(bf16[512,1024]{1,0:T(8,128)(2,1)S(1)} %copy-done.16), channel_id=1, source_target_pairs={{0,1},{3,2},{4,5},{7,6},{8,9},{11,10},{12,13},{15,14},{16,17},{19,... | collective-permute-start | bytes 3145736 | tf_op jit(solution)/shard_map/ppermute | solution.py:464
  278.7 0.8 pad_maximum_fusion.1
  279.6 6.1 %input_grad.12 = bf16[512,1024]{1,0:T(8,128)(2,1)} custom-call(s32[1]{0:T(128)} %bitcast.17.pick_ref, bf16[512,768]{1,0:T(8,128)(2,1)} %copy-done, bf16[512,768]{1,0:T(8,128)(2,1)} %copy-done.1, bf16[3,1024,256]{2,1,0:T(8,128)(2,1)} %copy-done.10, bf16[3,1024,256]{2,1,0:T(8,128)(2,1)} %collective-permute-done.6.refs_1_.refs_3_, ...), custom_call_target="tpu_custom_call" | custom-call | flops 1610612736 | bytes 5767168 | tf_op jit(solution)/shard_map/input_grad/pallas_call | solution.py:303
  285.7 6.1 %input_grad.8 = bf16[512,1024]{1,0:T(8,128)(2,1)} custom-call(s32[1]{0:T(128)} %bitcast.10.pick_ref, bf16[512,768]{1,0:T(8,128)(2,1)} %copy-done, bf16[512,768]{1,0:T(8,128)(2,1)} %copy-done.1, bf16[3,1024,256]{2,1,0:T(8,128)(2,1)} %copy-done.10, bf16[3,1024,256]{2,1,0:T(8,128)(2,1)} %collective-permute-done.6.refs_1_.refs_3_, ...), custom_call_target="tpu_custom_call" | custom-call | flops 1610612736 | bytes 5767168 | tf_op jit(solution)/shard_map/input_grad/pallas_call | solution.py:303
  291.8 3.2 %add_convert_fusion = bf16[512,1024]{1,0:T(8,128)(2,1)S(1)} fusion(bf16[512,1024]{1,0:T(8,128)(2,1)} %collective-permute-done.29, bf16[512,1024]{1,0:T(8,128)(2,1)} %collective-permute-done.27, bf16[512,1024]{1,0:T(8,128)(2,1)} %collective-permute-done.26, bf16[512,1024]{1,0:T(8,128)(2,1)} %input_grad.12), kind=kLoop, calls=%fused_computation.1 | loop fusion | flops 4194304 | bytes 5242880 | tf_op jit(solution)/shard_map/convert_element_type | solution.py:459
  295.0 9.7 %collective-permute-done.20 = bf16[512,1024]{1,0:T(8,128)(2,1)} collective-permute-done((bf16[512,1024]{1,0:T(8,128)(2,1)S(1)}, bf16[512,1024]{1,0:T(8,128)(2,1)}, u32[]{:S(2)}, u32[]{:S(2)}) %collective-permute-start.20) | collective-permute-done | bytes 1048608 | tf_op jit(solution)/shard_map/ppermute | solution.py:464
  304.7 2.8 add_convert_fusion.4
  307.5 1.5 pad_maximum_fusion
  (86 shorter events, 6.1 us)
Async XLA Ops:
  2.7 67.9 %copy-start.10 = (bf16[3,1024,256]{2,1,0:T(8,128)(2,1)}, bf16[3,1024,256]{2,1,0:T(8,128)(2,1)S(1)}, u32[]{:S(2)}) copy-start(bf16[3,1024,256]{2,1,0:T(8,128)(2,1)S(1)} %get-tuple-element.44.refs_0_.refs_2_) | copy-start | bytes 4718596
  2.7 67.9 %copy-start.11 = (bf16[3,1024,256]{2,1,0:T(8,128)(2,1)}, bf16[3,1024,256]{2,1,0:T(8,128)(2,1)S(1)}, u32[]{:S(2)}) copy-start(bf16[3,1024,256]{2,1,0:T(8,128)(2,1)S(1)} %get-tuple-element.27.refs_0_.refs_12_) | copy-start | bytes 4718596
  2.7 47.3 %copy-start.21 = (f32[16,512]{1,0:T(8,128)S(1)}, f32[16,512]{1,0:T(8,128)}, u32[]{:S(2)}) copy-start(f32[16,512]{1,0:T(8,128)} %param.10) | copy-start | bytes 98308
  2.8 47.3 %copy-start.22 = (f32[16,512]{1,0:T(8,128)S(1)}, f32[16,512]{1,0:T(8,128)}, u32[]{:S(2)}) copy-start(f32[16,512]{1,0:T(8,128)} %param.9) | copy-start | bytes 98308
  2.8 37.5 %collective-permute-start = (bf16[3,1024,256]{2,1,0:T(8,128)(2,1)S(1)}, bf16[3,1024,256]{2,1,0:T(8,128)(2,1)}, u32[]{:S(2)}, u32[]{:S(2)}) collective-permute-start(bf16[3,1024,256]{2,1,0:T(8,128)(2,1)S(1)} %get-tuple-element.44.refs_0_.refs_2_), channel_id=1, source_target_pairs={{0,8},{4,12},{8,0},{12,4},{16,24},{20,28},{24,16},{28,20},{1,9},{5... | collective-permute-start | bytes 4718600 | tf_op jit(solution)/shard_map/ppermute | solution.py:326
  5.8 36.0 %collective-permute-start.2 = (bf16[3,1024,256]{2,1,0:T(8,128)(2,1)S(1)}, bf16[3,1024,256]{2,1,0:T(8,128)(2,1)}, u32[]{:S(2)}, u32[]{:S(2)}) collective-permute-start(bf16[3,1024,256]{2,1,0:T(8,128)(2,1)S(1)} %get-tuple-element.44.refs_0_.refs_2_), channel_id=1, source_target_pairs={{0,16},{4,20},{8,24},{12,28},{16,0},{20,4},{24,8},{28,12},{1,17},{... | collective-permute-start | bytes 4718600 | tf_op jit(solution)/shard_map/ppermute | solution.py:326
  7.3 40.9 %collective-permute-start.6 = (bf16[3,1024,256]{2,1,0:T(8,128)(2,1)S(1)}, bf16[3,1024,256]{2,1,0:T(8,128)(2,1)}, u32[]{:S(2)}, u32[]{:S(2)}) collective-permute-start(bf16[3,1024,256]{2,1,0:T(8,128)(2,1)S(1)} %get-tuple-element.44.refs_0_.refs_2_), channel_id=1, source_target_pairs={{0,4},{4,0},{8,12},{12,8},{16,20},{20,16},{24,28},{28,24},{1,5},{5... | collective-permute-start | bytes 4718600 | tf_op jit(solution)/shard_map/ppermute | solution.py:326
  40.3 7.9 %collective-permute-start.7 = (bf16[3,1024,256]{2,1,0:T(8,128)(2,1)}, bf16[3,1024,256]{2,1,0:T(8,128)(2,1)}, u32[]{:S(2)}, u32[]{:S(2)}) collective-permute-start(bf16[3,1024,256]{2,1,0:T(8,128)(2,1)} %collective-permute-done.refs_2_.refs_4_), channel_id=1, source_target_pairs={{0,4},{4,0},{8,12},{12,8},{16,20},{20,16},{24,28},{28,24},{1,5},{5... | collective-permute-start | bytes 4718600 | tf_op jit(solution)/shard_map/ppermute | solution.py:326
  41.7 6.5 %collective-permute-start.8 = (bf16[3,1024,256]{2,1,0:T(8,128)(2,1)}, bf16[3,1024,256]{2,1,0:T(8,128)(2,1)}, u32[]{:S(2)}, u32[]{:S(2)}) collective-permute-start(bf16[3,1024,256]{2,1,0:T(8,128)(2,1)} %collective-permute-done.2.refs_4_.refs_6_), channel_id=1, source_target_pairs={{0,4},{4,0},{8,12},{12,8},{16,20},{20,16},{24,28},{28,24},{1,5},{5... | collective-permute-start | bytes 4718600 | tf_op jit(solution)/shard_map/ppermute | solution.py:326
  43.8 20.7 %collective-permute-start.1 = (bf16[3,512,256]{2,1,0:T(8,128)(2,1)}, bf16[3,512,256]{2,1,0:T(8,128)(2,1)}, u32[]{:S(2)}, u32[]{:S(2)}) collective-permute-start(bf16[3,512,256]{2,1,0:T(8,128)(2,1)} %slice.87), channel_id=1, source_target_pairs={{0,16},{4,20},{8,24},{12,28},{16,0},{20,4},{24,8},{28,12},{1,17},{... | collective-permute-start | bytes 2359304 | tf_op jit(solution)/shard_map/ppermute | solution.py:326
  47.4 20.7 %collective-permute-start.3 = (bf16[3,512,256]{2,1,0:T(8,128)(2,1)}, bf16[3,512,256]{2,1,0:T(8,128)(2,1)}, u32[]{:S(2)}, u32[]{:S(2)}) collective-permute-start(bf16[3,512,256]{2,1,0:T(8,128)(2,1)} %slice.88), channel_id=1, source_target_pairs={{0,8},{4,12},{8,0},{12,4},{16,24},{20,28},{24,16},{28,20},{1,9},{5... | collective-permute-start | bytes 2359304 | tf_op jit(solution)/shard_map/ppermute | solution.py:326
  48.2 56.4 %collective-permute-start.9 = (bf16[3,1024,256]{2,1,0:T(8,128)(2,1)S(1)}, bf16[3,1024,256]{2,1,0:T(8,128)(2,1)}, u32[]{:S(2)}, u32[]{:S(2)}) collective-permute-start(bf16[3,1024,256]{2,1,0:T(8,128)(2,1)S(1)} %get-tuple-element.27.refs_0_.refs_12_), channel_id=1, source_target_pairs={{0,8},{4,12},{8,0},{12,4},{16,24},{20,28},{24,16},{28,20},{1,9},{5... | collective-permute-start | bytes 4718600 | tf_op jit(solution)/shard_map/ppermute | solution.py:326
  49.5 55.5 %collective-permute-start.10 = (bf16[3,1024,256]{2,1,0:T(8,128)(2,1)S(1)}, bf16[3,1024,256]{2,1,0:T(8,128)(2,1)}, u32[]{:S(2)}, u32[]{:S(2)}) collective-permute-start(bf16[3,1024,256]{2,1,0:T(8,128)(2,1)S(1)} %get-tuple-element.27.refs_0_.refs_12_), channel_id=1, source_target_pairs={{0,16},{4,20},{8,24},{12,28},{16,0},{20,4},{24,8},{28,12},{1,17},{... | collective-permute-start | bytes 4718600 | tf_op jit(solution)/shard_map/ppermute | solution.py:326
  64.4 19.7 %collective-permute-start.4 = (bf16[3,512,256]{2,1,0:T(8,128)(2,1)}, bf16[3,512,256]{2,1,0:T(8,128)(2,1)}, u32[]{:S(2)}, u32[]{:S(2)}) collective-permute-start(bf16[3,512,256]{2,1,0:T(8,128)(2,1)} %collective-permute-done.1.refs_0_.refs_8_), channel_id=1, source_target_pairs={{0,4},{4,0},{8,12},{12,8},{16,20},{20,16},{24,28},{28,24},{1,5},{5... | collective-permute-start | bytes 2359304 | tf_op jit(solution)/shard_map/ppermute | solution.py:326
  68.1 16.0 %collective-permute-start.5 = (bf16[3,512,256]{2,1,0:T(8,128)(2,1)}, bf16[3,512,256]{2,1,0:T(8,128)(2,1)}, u32[]{:S(2)}, u32[]{:S(2)}) collective-permute-start(bf16[3,512,256]{2,1,0:T(8,128)(2,1)} %collective-permute-done.3.refs_1_.refs_9_), channel_id=1, source_target_pairs={{0,4},{4,0},{8,12},{12,8},{16,20},{20,16},{24,28},{28,24},{1,5},{5... | collective-permute-start | bytes 2359304 | tf_op jit(solution)/shard_map/ppermute | solution.py:326
  68.1 3.0 copy-start.23
  70.6 44.8 %collective-permute-start.13 = (bf16[3,1024,256]{2,1,0:T(8,128)(2,1)S(1)}, bf16[3,1024,256]{2,1,0:T(8,128)(2,1)}, u32[]{:S(2)}, u32[]{:S(2)}) collective-permute-start(bf16[3,1024,256]{2,1,0:T(8,128)(2,1)S(1)} %get-tuple-element.27.refs_0_.refs_12_), channel_id=1, source_target_pairs={{0,4},{4,0},{8,12},{12,8},{16,20},{20,16},{24,28},{28,24},{1,5},{5... | collective-permute-start | bytes 4718600 | tf_op jit(solution)/shard_map/ppermute | solution.py:326
  93.5 17.0 %copy-start.24 = (f32[512]{0:T(512)S(1)}, f32[512]{0:T(512)}, u32[]{:S(2)}) copy-start(f32[512]{0:T(512)} %param.11) | copy-start | bytes 6148
  93.6 17.0 %copy-start.3 = (bf16[512,256]{1,0:T(8,128)(2,1)S(1)}, bf16[512,256]{1,0:T(8,128)(2,1)}, u32[]{:S(2)}) copy-start(bf16[512,256]{1,0:T(8,128)(2,1)} %get-tuple-element.47.refs_5_.g_ref) | copy-start | bytes 786436
  93.6 17.0 %copy-start.4 = (bf16[3,512,256]{2,1,0:T(8,128)(2,1)S(1)}, bf16[3,512,256]{2,1,0:T(8,128)(2,1)}, u32[]{:S(2)}) copy-start(bf16[3,512,256]{2,1,0:T(8,128)(2,1)} %get-tuple-element.23.proj_ref) | copy-start | bytes 2359300
  93.6 16.9 %copy-start.7 = (f32[4,16,256]{2,1,0:T(8,128)S(1)}, f32[4,16,256]{2,1,0:T(8,128)}, u32[]{:S(2)}) copy-start(f32[4,16,256]{2,1,0:T(8,128)} %get-tuple-element.49.refs_6_.coef_ref) | copy-start | bytes 196612
  93.6 16.9 %copy-start.8 = (f32[2,2,128,128]{3,2,1,0:T(8,128)S(1)}, f32[2,2,128,128]{3,2,1,0:T(8,128)}, u32[]{:S(2)}) copy-start(f32[2,2,128,128]{3,2,1,0:T(8,128)} %get-tuple-element.24.runs_ref) | copy-start | bytes 786436
  104.6 10.8 %collective-permute-start.14 = (bf16[3,1024,256]{2,1,0:T(8,128)(2,1)}, bf16[3,1024,256]{2,1,0:T(8,128)(2,1)}, u32[]{:S(2)}, u32[]{:S(2)}) collective-permute-start(bf16[3,1024,256]{2,1,0:T(8,128)(2,1)} %collective-permute-done.9.refs_2_.refs_14_), channel_id=1, source_target_pairs={{0,4},{4,0},{8,12},{12,8},{16,20},{20,16},{24,28},{28,24},{1,5},{5... | collective-permute-start | bytes 4718600 | tf_op jit(solution)/shard_map/ppermute | solution.py:326
  105.1 10.4 %collective-permute-start.15 = (bf16[3,1024,256]{2,1,0:T(8,128)(2,1)}, bf16[3,1024,256]{2,1,0:T(8,128)(2,1)}, u32[]{:S(2)}, u32[]{:S(2)}) collective-permute-start(bf16[3,1024,256]{2,1,0:T(8,128)(2,1)} %collective-permute-done.10.refs_4_.refs_16_), channel_id=1, source_target_pairs={{0,4},{4,0},{8,12},{12,8},{16,20},{20,16},{24,28},{28,24},{1,5},{5... | collective-permute-start | bytes 4718600 | tf_op jit(solution)/shard_map/ppermute | solution.py:326
  108.4 20.2 %collective-permute-start.11 = (bf16[3,512,256]{2,1,0:T(8,128)(2,1)}, bf16[3,512,256]{2,1,0:T(8,128)(2,1)S(1)}, u32[]{:S(2)}, u32[]{:S(2)}) collective-permute-start(bf16[3,512,256]{2,1,0:T(8,128)(2,1)} %slice.92), channel_id=1, source_target_pairs={{0,16},{4,20},{8,24},{12,28},{16,0},{20,4},{24,8},{28,12},{1,17},{... | collective-permute-start | bytes 2359304 | tf_op jit(solution)/shard_map/ppermute | solution.py:326
  110.0 19.7 %collective-permute-start.12 = (bf16[3,512,256]{2,1,0:T(8,128)(2,1)S(1)}, bf16[3,512,256]{2,1,0:T(8,128)(2,1)}, u32[]{:S(2)}, u32[]{:S(2)}) collective-permute-start(bf16[3,512,256]{2,1,0:T(8,128)(2,1)S(1)} %slice.93), channel_id=1, source_target_pairs={{0,8},{4,12},{8,0},{12,4},{16,24},{20,28},{24,16},{28,20},{1,9},{5... | collective-permute-start | bytes 2359304 | tf_op jit(solution)/shard_map/ppermute | solution.py:326
  114.5 0.9 copy-start
  128.6 4.7 %copy-start.12 = (bf16[3,512,256]{2,1,0:T(8,128)(2,1)}, bf16[3,512,256]{2,1,0:T(8,128)(2,1)S(1)}, u32[]{:S(2)}) copy-start(bf16[3,512,256]{2,1,0:T(8,128)(2,1)S(1)} %collective-permute-done.11.refs_0_.refs_18_) | copy-start | bytes 2359300
  129.7 3.4 %collective-permute-start.16 = (bf16[3,512,256]{2,1,0:T(8,128)(2,1)S(1)}, bf16[3,512,256]{2,1,0:T(8,128)(2,1)S(1)}, u32[]{:S(2)}, u32[]{:S(2)}) collective-permute-start(bf16[3,512,256]{2,1,0:T(8,128)(2,1)S(1)} %collective-permute-done.11.refs_0_.refs_18_), channel_id=1, source_target_pairs={{0,4},{4,0},{8,12},{12,8},{16,20},{20,16},{24,28},{28,24},{1,5},{5... | collective-permute-start | bytes 2359304 | tf_op jit(solution)/shard_map/ppermute | solution.py:326
  129.7 3.6 %collective-permute-start.17 = (bf16[3,512,256]{2,1,0:T(8,128)(2,1)}, bf16[3,512,256]{2,1,0:T(8,128)(2,1)S(1)}, u32[]{:S(2)}, u32[]{:S(2)}) collective-permute-start(bf16[3,512,256]{2,1,0:T(8,128)(2,1)} %collective-permute-done.12.refs_1_.refs_19_), channel_id=1, source_target_pairs={{0,4},{4,0},{8,12},{12,8},{16,20},{20,16},{24,28},{28,24},{1,5},{5... | collective-permute-start | bytes 2359304 | tf_op jit(solution)/shard_map/ppermute | solution.py:326
  133.0 0.9 copy-start.13
  133.3 0.9 copy-start.14
  134.2 18.3 %copy-start.2 = (bf16[512,256]{1,0:T(8,128)(2,1)S(1)}, bf16[512,256]{1,0:T(8,128)(2,1)}, u32[]{:S(2)}) copy-start(bf16[512,256]{1,0:T(8,128)(2,1)} %get-tuple-element.46.refs_5_.g_ref) | copy-start | bytes 786436
  134.2 18.3 %copy-start.6 = (f32[4,16,256]{2,1,0:T(8,128)S(1)}, f32[4,16,256]{2,1,0:T(8,128)}, u32[]{:S(2)}) copy-start(f32[4,16,256]{2,1,0:T(8,128)} %get-tuple-element.48.refs_6_.coef_ref) | copy-start | bytes 196612
  152.5 1.1 copy-start.5
  153.7 0.9 copy-start.9
  158.6 0.9 copy-start.1
  165.7 27.3 %collective-permute-start.24 = (bf16[512,1024]{1,0:T(8,128)(2,1)}, bf16[512,1024]{1,0:T(8,128)(2,1)}, u32[]{:S(2)}, u32[]{:S(2)}) collective-permute-start(bf16[512,1024]{1,0:T(8,128)(2,1)} %input_grad.15), channel_id=1, source_target_pairs={{0,1},{3,2},{4,5},{7,6},{8,9},{11,10},{12,13},{15,14},{16,17},{19,... | collective-permute-start | bytes 3145736 | tf_op jit(solution)/shard_map/ppermute | solution.py:464
  170.2 22.8 %copy-start.20 = (bf16[512,1024]{1,0:T(8,128)(2,1)S(1)}, bf16[512,1024]{1,0:T(8,128)(2,1)}, u32[]{:S(2)}) copy-start(bf16[512,1024]{1,0:T(8,128)(2,1)} %input_grad.15) | copy-start | bytes 3145732
  176.4 39.1 %collective-permute-start.18 = (bf16[512,1024]{1,0:T(8,128)(2,1)}, bf16[512,1024]{1,0:T(8,128)(2,1)}, u32[]{:S(2)}, u32[]{:S(2)}) collective-permute-start(bf16[512,1024]{1,0:T(8,128)(2,1)} %input_grad.11), channel_id=1, source_target_pairs={{0,1},{3,2},{4,5},{7,6},{8,9},{11,10},{12,13},{15,14},{16,17},{19,... | collective-permute-start | bytes 3145736 | tf_op jit(solution)/shard_map/ppermute | solution.py:464
  194.6 44.7 %collective-permute-start.28 = (bf16[512,1024]{1,0:T(8,128)(2,1)S(1)}, bf16[512,1024]{1,0:T(8,128)(2,1)}, u32[]{:S(2)}, u32[]{:S(2)}) collective-permute-start(bf16[512,1024]{1,0:T(8,128)(2,1)S(1)} %add_convert_fusion.2), channel_id=1, source_target_pairs={{1,2},{2,1},{5,6},{6,5},{9,10},{10,9},{13,14},{14,13},{17,18},{18,... | collective-permute-start | bytes 3145736 | tf_op jit(solution)/shard_map/ppermute | solution.py:464
  197.5 18.0 %copy-start.19 = (bf16[512,1024]{1,0:T(8,128)(2,1)S(1)}, bf16[512,1024]{1,0:T(8,128)(2,1)}, u32[]{:S(2)}) copy-start(bf16[512,1024]{1,0:T(8,128)(2,1)} %input_grad.11) | copy-start | bytes 3145732
  203.7 45.6 %collective-permute-start.25 = (bf16[512,1024]{1,0:T(8,128)(2,1)}, bf16[512,1024]{1,0:T(8,128)(2,1)}, u32[]{:S(2)}, u32[]{:S(2)}) collective-permute-start(bf16[512,1024]{1,0:T(8,128)(2,1)} %input_grad.14), channel_id=1, source_target_pairs={{0,1},{3,2},{4,5},{7,6},{8,9},{11,10},{12,13},{15,14},{16,17},{19,... | collective-permute-start | bytes 3145736 | tf_op jit(solution)/shard_map/ppermute | solution.py:464
  218.1 43.3 %collective-permute-start.22 = (bf16[512,1024]{1,0:T(8,128)(2,1)}, bf16[512,1024]{1,0:T(8,128)(2,1)}, u32[]{:S(2)}, u32[]{:S(2)}) collective-permute-start(bf16[512,1024]{1,0:T(8,128)(2,1)} %add_convert_fusion.6), channel_id=1, source_target_pairs={{1,2},{2,1},{5,6},{6,5},{9,10},{10,9},{13,14},{14,13},{17,18},{18,... | collective-permute-start | bytes 3145736 | tf_op jit(solution)/shard_map/ppermute | solution.py:464
  225.9 13.4 %copy-start.15 = (bf16[512,1024]{1,0:T(8,128)(2,1)S(1)}, bf16[512,1024]{1,0:T(8,128)(2,1)}, u32[]{:S(2)}) copy-start(bf16[512,1024]{1,0:T(8,128)(2,1)} %input_grad.13) | copy-start | bytes 3145732
  232.1 33.2 %collective-permute-start.19 = (bf16[512,1024]{1,0:T(8,128)(2,1)}, bf16[512,1024]{1,0:T(8,128)(2,1)}, u32[]{:S(2)}, u32[]{:S(2)}) collective-permute-start(bf16[512,1024]{1,0:T(8,128)(2,1)} %input_grad.10), channel_id=1, source_target_pairs={{0,1},{3,2},{4,5},{7,6},{8,9},{11,10},{12,13},{15,14},{16,17},{19,... | collective-permute-start | bytes 3145736 | tf_op jit(solution)/shard_map/ppermute | solution.py:464
  241.9 27.7 %collective-permute-start.29 = (bf16[512,1024]{1,0:T(8,128)(2,1)}, bf16[512,1024]{1,0:T(8,128)(2,1)}, u32[]{:S(2)}, u32[]{:S(2)}) collective-permute-start(bf16[512,1024]{1,0:T(8,128)(2,1)} %add_convert_fusion.1), channel_id=1, source_target_pairs={{1,0},{2,3},{5,4},{6,7},{9,8},{10,11},{13,12},{14,15},{17,16},{18,... | collective-permute-start | bytes 3145736 | tf_op jit(solution)/shard_map/ppermute | solution.py:464
  249.4 12.0 %copy-start.16 = (bf16[512,1024]{1,0:T(8,128)(2,1)S(1)}, bf16[512,1024]{1,0:T(8,128)(2,1)}, u32[]{:S(2)}) copy-start(bf16[512,1024]{1,0:T(8,128)(2,1)} %input_grad.9) | copy-start | bytes 3145732
  252.4 12.9 %copy-start.18 = (bf16[512,1024]{1,0:T(8,128)(2,1)S(1)}, bf16[512,1024]{1,0:T(8,128)(2,1)}, u32[]{:S(2)}) copy-start(bf16[512,1024]{1,0:T(8,128)(2,1)} %input_grad.10) | copy-start | bytes 3145732
  252.4 39.4 %collective-permute-start.27 = (bf16[512,1024]{1,0:T(8,128)(2,1)}, bf16[512,1024]{1,0:T(8,128)(2,1)}, u32[]{:S(2)}, u32[]{:S(2)}) collective-permute-start(bf16[512,1024]{1,0:T(8,128)(2,1)} %add_convert_fusion.3), channel_id=1, source_target_pairs={{1,2},{2,1},{5,6},{6,5},{9,10},{10,9},{13,14},{14,13},{17,18},{18,... | collective-permute-start | bytes 3145736 | tf_op jit(solution)/shard_map/ppermute | solution.py:464
  254.2 37.6 %collective-permute-start.26 = (bf16[512,1024]{1,0:T(8,128)(2,1)S(1)}, bf16[512,1024]{1,0:T(8,128)(2,1)}, u32[]{:S(2)}, u32[]{:S(2)}) collective-permute-start(bf16[512,1024]{1,0:T(8,128)(2,1)S(1)} %copy-done.15), channel_id=1, source_target_pairs={{0,1},{3,2},{4,5},{7,6},{8,9},{11,10},{12,13},{15,14},{16,17},{19,... | collective-permute-start | bytes 3145736 | tf_op jit(solution)/shard_map/ppermute | solution.py:464
  264.0 31.0 %collective-permute-start.23 = (bf16[512,1024]{1,0:T(8,128)(2,1)}, bf16[512,1024]{1,0:T(8,128)(2,1)}, u32[]{:S(2)}, u32[]{:S(2)}) collective-permute-start(bf16[512,1024]{1,0:T(8,128)(2,1)} %add_convert_fusion.5), channel_id=1, source_target_pairs={{1,0},{2,3},{5,4},{6,7},{9,8},{10,11},{13,12},{14,15},{17,16},{18,... | collective-permute-start | bytes 3145736 | tf_op jit(solution)/shard_map/ppermute | solution.py:464
  268.0 27.0 %collective-permute-start.21 = (bf16[512,1024]{1,0:T(8,128)(2,1)}, bf16[512,1024]{1,0:T(8,128)(2,1)}, u32[]{:S(2)}, u32[]{:S(2)}) collective-permute-start(bf16[512,1024]{1,0:T(8,128)(2,1)} %add_convert_fusion.7), channel_id=1, source_target_pairs={{1,2},{2,1},{5,6},{6,5},{9,10},{10,9},{13,14},{14,13},{17,18},{18,... | collective-permute-start | bytes 3145736 | tf_op jit(solution)/shard_map/ppermute | solution.py:464
  269.6 35.1 %collective-permute-start.20 = (bf16[512,1024]{1,0:T(8,128)(2,1)S(1)}, bf16[512,1024]{1,0:T(8,128)(2,1)}, u32[]{:S(2)}, u32[]{:S(2)}) collective-permute-start(bf16[512,1024]{1,0:T(8,128)(2,1)S(1)} %copy-done.16), channel_id=1, source_target_pairs={{0,1},{3,2},{4,5},{7,6},{8,9},{11,10},{12,13},{15,14},{16,17},{19,... | collective-permute-start | bytes 3145736 | tf_op jit(solution)/shard_map/ppermute | solution.py:464
  291.8 12.9 %copy-start.17 = (bf16[512,1024]{1,0:T(8,128)(2,1)S(1)}, bf16[512,1024]{1,0:T(8,128)(2,1)}, u32[]{:S(2)}) copy-start(bf16[512,1024]{1,0:T(8,128)(2,1)} %input_grad.8) | copy-start | bytes 3145732
